TPU v7x, 256 devices: a whole 4x4x8 slice. The times are simulated.
256 devices in a mesh: ctx: 16 (over x_lo, z), head: 16 (over x_hi, y, core).
Axes of the slice: x: 4 (x_hi: 2, x_lo: 2; x = x_hi * 2 + x_lo), y: 4, z: 8, core: 2. Of those that a mesh axis runs over, the one named last changes fastest.
Arguments:
- queries: bfloat16 [6144, 4, 4096], P(('ctx', 'head')), may hold values from -84 to 84
- key_states: bfloat16 [6144, 4, 4096], P(('ctx', 'head')), may hold values from -4 to 4
- value_states: bfloat16 [6144, 4, 4096], P(('ctx', 'head')), may hold values from -6 to 6
- out_grad: bfloat16 [6144, 4096], P(('ctx', 'head')), may hold values from -6 to 6
- offsets: int32 [32], replicated, may hold values from 0 to 3
- block_mask: int32 [12, 12], replicated, may hold values from 0 to 1, as said below
Outputs:
- attended: bfloat16 [6144, 4096], P(('ctx', 'head'))
- query_grad: bfloat16 [6144, 4096], P(('ctx', 'head'))
- key_grad: bfloat16 [6144, 4096], P(('ctx', 'head'))
- value_grad: bfloat16 [6144, 4096], P(('ctx', 'head'))
Inputs may be any that keep to these rules, and one draw needn't show every extreme that they name: block_mask is 1 on its diagonal and 0 above it.
All inputs are finite; a program needn't handle non-finite values.
Results may differ from a plain program's by a relative error of at most 0.015.
Values may be sent and summed in bfloat16 or wider, within the bound.
A program may use at most 128 MiB of HBM per device.

v0:
```python
import jax
import jax.numpy as jnp
from jax import lax
from jax.sharding import PartitionSpec as P

HEADS = 32
HD = 128
BLK = 512


def select_heads(states, offsets, head_count):
    row_count = states.shape[0]
    res_count = states.shape[1]
    head_size = states.shape[2] // head_count
    split_view = states.reshape(row_count, res_count, head_count, head_size)
    chosen = jnp.arange(res_count, dtype=jnp.int32)[:, None] == offsets[None, :]
    picked = jnp.sum(
        jnp.where(chosen[None, :, :, None], split_view, jnp.zeros_like(split_view)), axis=1
    )
    return picked.reshape(row_count, head_count * head_size)


def block_allow(query_index, key_index, block_mask):
    block_count = block_mask.shape[0]
    block_ids = jnp.arange(block_count, dtype=jnp.int32)[None, :]
    query_hot = (query_index[:, None] // BLK == block_ids).astype(jnp.float32)
    key_hot = (key_index[:, None] // BLK == block_ids).astype(jnp.float32)
    listed = jnp.dot(jnp.dot(query_hot, block_mask.astype(jnp.float32)), key_hot.T) > 0.5
    return listed & (key_index[None, :] <= query_index[:, None])


def grads_block(
    query_heads, grad_heads, key_blk, value_blk, log_sum, row_dot, allowed, scale_factor
):
    scores = (
        jnp.einsum("qhd,khd->hqk", query_heads, key_blk, preferred_element_type=jnp.float32)
        * scale_factor
    )
    prob_bf = jnp.exp(jnp.where(allowed[None], scores - log_sum[:, :, None], -jnp.inf)).astype(
        jnp.bfloat16
    )
    prob_grad = jnp.einsum(
        "qhd,khd->hqk", grad_heads, value_blk, preferred_element_type=jnp.float32
    )
    score_grad = (
        prob_bf.astype(jnp.float32) * (prob_grad - row_dot[:, :, None]) * scale_factor
    ).astype(jnp.bfloat16)
    return (prob_bf, score_grad)


def on_device(queries, key_states, value_states, out_grad, offsets, block_mask):
    head_ways = lax.axis_size("head")
    head_local = HEADS // head_ways
    head_size = HD
    whole_q, whole_k, whole_v, whole_g = (
        lax.all_to_all(queries, "head", split_axis=2, concat_axis=0, tiled=True),
        lax.all_to_all(key_states, "head", split_axis=2, concat_axis=0, tiled=True),
        lax.all_to_all(value_states, "head", split_axis=2, concat_axis=0, tiled=True),
        lax.all_to_all(out_grad[:, None, :], "head", split_axis=2, concat_axis=0, tiled=True),
    )
    local_offsets = lax.dynamic_slice_in_dim(
        offsets, lax.axis_index("head") * head_local, head_local, 0
    )
    query_loc = select_heads(whole_q, local_offsets, head_local)
    key_loc = select_heads(whole_k, local_offsets, head_local)
    value_loc = select_heads(whole_v, local_offsets, head_local)
    grad_loc = whole_g[:, 0, :]
    local_rows = query_loc.shape[0]
    local_width = head_local * head_size
    query_index = lax.axis_index("ctx") * local_rows + jnp.arange(local_rows, dtype=jnp.int32)
    key_all, value_all = (
        lax.all_gather(key_loc, "ctx", axis=0, tiled=True),
        lax.all_gather(value_loc, "ctx", axis=0, tiled=True),
    )
    block_count = key_all.shape[0] // BLK
    scale_factor = head_size ** (-0.5)
    query_heads = query_loc.reshape(local_rows, head_local, head_size)
    grad_heads = grad_loc.reshape(local_rows, head_local, head_size)
    block_steps = jnp.arange(block_count, dtype=jnp.int32)

    def key_block(block_idx):
        start_row = block_idx * BLK
        key_blk = lax.dynamic_slice_in_dim(key_all, start_row, BLK, 0).reshape(
            BLK, head_local, head_size
        )
        value_blk = lax.dynamic_slice_in_dim(value_all, start_row, BLK, 0).reshape(
            BLK, head_local, head_size
        )
        allowed = block_allow(query_index, start_row + jnp.arange(BLK, dtype=jnp.int32), block_mask)
        return (key_blk, value_blk, allowed)

    def stats_step(running, block_idx):
        key_blk, value_blk, allowed = key_block(block_idx)

        def stats_live(state):
            row_max, row_sum = state
            scores = (
                jnp.einsum("qhd,khd->hqk", query_heads, key_blk, preferred_element_type=jnp.float32)
                * scale_factor
            )
            new_max = jnp.maximum(row_max, jnp.max(jnp.where(allowed[None], scores, -1e30), axis=2))
            weights = jnp.exp(jnp.where(allowed[None], scores - new_max[:, :, None], -jnp.inf))
            new_sum = row_sum * jnp.exp(row_max - new_max) + jnp.sum(weights, axis=2)
            return (new_max, new_sum)

        return (lax.cond(jnp.any(allowed), stats_live, lambda state: state, running), None)

    start_max = jnp.full((head_local, local_rows), -1e30, jnp.float32)
    start_sum = jnp.zeros((head_local, local_rows), jnp.float32)
    zero_heads = jnp.zeros((local_rows, head_local, head_size), jnp.float32)
    (row_max, row_sum), _ = lax.scan(stats_step, (start_max, start_sum), block_steps)
    log_sum = row_max + jnp.log(row_sum)

    def output_step(running, block_idx):
        key_blk, value_blk, allowed = key_block(block_idx)

        def output_live(total_out):
            scores = (
                jnp.einsum("qhd,khd->hqk", query_heads, key_blk, preferred_element_type=jnp.float32)
                * scale_factor
            )
            prob_bf = jnp.exp(
                jnp.where(allowed[None], scores - log_sum[:, :, None], -jnp.inf)
            ).astype(jnp.bfloat16)
            return total_out + jnp.einsum(
                "hqk,khd->qhd", prob_bf, value_blk, preferred_element_type=jnp.float32
            )

        return (lax.cond(jnp.any(allowed), output_live, lambda total_out: total_out, running), None)

    accum_out, _ = lax.scan(output_step, zero_heads, block_steps)
    attended = accum_out.astype(jnp.bfloat16)
    row_dot = jnp.sum(grad_heads.astype(jnp.float32) * attended.astype(jnp.float32), axis=2).T
    empty_block = jnp.zeros((BLK, local_width), jnp.float32)

    def backward_step(running, block_idx):
        key_blk, value_blk, allowed = key_block(block_idx)

        def backward_live(total_grad):
            prob_bf, score_grad = grads_block(
                query_heads, grad_heads, key_blk, value_blk, log_sum, row_dot, allowed, scale_factor
            )
            next_grad = total_grad + jnp.einsum(
                "hqk,khd->qhd", score_grad, key_blk, preferred_element_type=jnp.float32
            )
            key_term = jnp.einsum(
                "hqk,qhd->khd", score_grad, query_heads, preferred_element_type=jnp.float32
            )
            value_term = jnp.einsum(
                "hqk,qhd->khd", prob_bf, grad_heads, preferred_element_type=jnp.float32
            )
            return (
                next_grad,
                key_term.reshape(BLK, local_width),
                value_term.reshape(BLK, local_width),
            )

        def dead(total_grad):
            return (total_grad, empty_block, empty_block)

        next_grad, key_term, value_term = lax.cond(jnp.any(allowed), backward_live, dead, running)
        return (next_grad, (key_term, value_term))

    accum_query, (key_blocks, value_blocks) = lax.scan(backward_step, zero_heads, block_steps)
    query_grad = accum_query.astype(jnp.bfloat16).reshape(local_rows, local_width)
    key_whole = key_blocks.reshape(block_count * BLK, local_width)
    value_whole = value_blocks.reshape(block_count * BLK, local_width)
    key_summed, value_summed = (
        lax.psum_scatter(key_whole, "ctx", scatter_dimension=0, tiled=True),
        lax.psum_scatter(value_whole, "ctx", scatter_dimension=0, tiled=True),
    )
    key_grad = key_summed.astype(jnp.bfloat16)
    value_grad = value_summed.astype(jnp.bfloat16)
    attended_rows = attended.reshape(local_rows, local_width)
    attended_out, query_out, key_out, value_out = (
        lax.all_to_all(attended_rows, "head", split_axis=0, concat_axis=1, tiled=True),
        lax.all_to_all(query_grad, "head", split_axis=0, concat_axis=1, tiled=True),
        lax.all_to_all(key_grad, "head", split_axis=0, concat_axis=1, tiled=True),
        lax.all_to_all(value_grad, "head", split_axis=0, concat_axis=1, tiled=True),
    )
    return (attended_out, query_out, key_out, value_out)


def solution(mesh):
    in_specs = (
        P(("ctx", "head"), None, None),
        P(("ctx", "head"), None, None),
        P(("ctx", "head"), None, None),
        P(("ctx", "head"), None),
        P(),
        P(),
    )
    out_specs = (
        P(("ctx", "head"), None),
        P(("ctx", "head"), None),
        P(("ctx", "head"), None),
        P(("ctx", "head"), None),
    )
    return jax.shard_map(
        on_device, mesh=mesh, in_specs=in_specs, out_specs=out_specs, check_vma=False
    )
```

profile of v0, /device:TPU:1, one launch (start us, length us, event | category | flops | bytes accessed | tf_op | source)
XLA Modules:
  0.0 667.3 jit_solution(5597181198400994462)
XLA Ops:
  7.2 6.5 copy.194
  13.7 7.3 %reshape.441 = bf16[16,2,12288]{2,1,0:T(2,128)(2,1)} reshape(bf16[4096,4,24]{2,1,0:T(4,128)(2,1)} %bitcast.156) | data formatting | bytes 1572864
  21.0 8.6 %all-to-all-start = ((bf16[16,2,12288]{2,1,0:T(2,128)(2,1)}), bf16[16,2,12288]{2,1,0:T(2,128)(2,1)S(1)}, u32[]{:S(2)}, u32[]{:S(2)}) async-start(bf16[16,2,12288]{2,1,0:T(2,128)(2,1)} %reshape.441), calls=%async_computation | async-start | bytes 1572864 | tf_op jit(solution)/shard_map/all_to_all | solution.py:57
  29.5 4.8 copy.197
  34.3 7.3 %reshape.439 = bf16[16,2,12288]{2,1,0:T(2,128)(2,1)} reshape(bf16[4096,4,24]{2,1,0:T(4,128)(2,1)} %bitcast.157) | data formatting | bytes 1572864
  43.9 5.0 all-to-all-start.1
  49.0 4.8 copy.202
  53.7 7.3 %reshape.437 = bf16[16,2,12288]{2,1,0:T(2,128)(2,1)} reshape(bf16[4096,4,24]{2,1,0:T(4,128)(2,1)} %bitcast.158) | data formatting | bytes 1572864
  63.4 5.0 all-to-all-start.2
  68.9 6.9 %reshape.442 = bf16[4096,4,24]{2,1,0:T(4,128)(2,1)} reshape(bf16[16,2,12288]{2,1,0:T(2,128)(2,1)S(1)} %all-to-all-done) | data formatting | bytes 1572864
  75.7 4.8 copy.195
  80.5 6.9 %reshape.440 = bf16[4096,4,24]{2,1,0:T(4,128)(2,1)} reshape(bf16[16,2,12288]{2,1,0:T(2,128)(2,1)S(1)} %all-to-all-done.1) | data formatting | bytes 1572864
  87.4 4.8 copy.198
  92.2 6.9 %reshape.438 = bf16[4096,4,24]{2,1,0:T(4,128)(2,1)} reshape(bf16[16,2,12288]{2,1,0:T(2,128)(2,1)S(1)} %all-to-all-done.2) | data formatting | bytes 1572864
  99.1 4.8 copy.203
  108.6 22.6 %reduce.9 = bf16[4096,24]{1,0:T(8,128)(2,1)S(1)} reduce(bf16[4096,1,24]{2,1,0:T(2,128)(2,1)S(1)} %bitcast.159, bf16[]{:T(256)} %broadcast.645), dimensions={1}, to_apply=%bitcast.115.reduce_sub_computation | reduce | bytes 393218
  133.3 7.2 %all-to-all-start.4 = ((bf16[16,2,3072]{2,1,0:T(2,128)(2,1)}), bf16[16,2,3072]{2,1,0:T(2,128)(2,1)S(1)}, u32[]{:S(2)}, u32[]{:S(2)}) async-start(bf16[16,2,3072]{2,1,0:T(2,128)(2,1)} %reshape.443), calls=%async_computation.4 | async-start | bytes 393216 | tf_op jit(solution)/shard_map/all_to_all | solution.py:59
  142.2 9.6 %all-to-all-done.4 = bf16[16,2,3072]{2,1,0:T(2,128)(2,1)S(1)} async-done(((bf16[16,2,3072]{2,1,0:T(2,128)(2,1)}), bf16[16,2,3072]{2,1,0:T(2,128)(2,1)S(1)}, u32[]{:S(2)}, u32[]{:S(2)}) %all-to-all-start.4) | async-done | bytes 196640 | tf_op jit(solution)/shard_map/all_to_all | solution.py:59
  159.5 14.5 %all-gather.3.cloned.1.call-done = bf16[6144,256]{1,0:T(8,128)(2,1)} async-done(((bf16[384,256]{1,0:T(8,128)(2,1)}), bf16[6144,256]{1,0:T(8,128)(2,1)}) %all-gather.3.cloned.1.call-update) | async-done | bytes 3145744 | tf_op jit(solution)/shard_map/all_gather | solution.py:72
  177.2 46.3 %while.60 = (s32[]{:T(128)}, f32[2,384]{1,0:T(2,128)S(1)}, f32[2,384]{1,0:T(2,128)S(1)}, s32[12]{0:T(128)S(1)}, bf16[384,12]{0,1:T(8,128)(2,1)}, /*index=5*/bf16...) while((s32[]{:T(128)}, f32[2,384]{1,0:T(2,128)S(1)}, ...), condition=%wide.region_9.10_spmd.clone, body=%wide.region_3.9_spmd.clone.sunk | while | flops 108543872 | bytes 4779273 | solution.py:111
  223.5 25.2 %all-gather.5.cloned.1.call-done = bf16[6144,256]{1,0:T(8,128)(2,1)} async-done(((bf16[384,256]{1,0:T(8,128)(2,1)}), bf16[6144,256]{1,0:T(8,128)(2,1)}) %all-gather.5.cloned.1.call-update) | async-done | bytes 3145744 | tf_op jit(solution)/shard_map/all_gather | solution.py:73
  248.6 4.8 copy.207
  254.2 56.7 %while.61 = (s32[]{:T(128)}, f32[384,2,128]{2,0,1:T(8,128)}, s32[12]{0:T(128)S(1)}, bf16[384,12]{0,1:T(8,128)(2,1)}, bf16[6144,256]{0,1:T(8,128)(2,1)S(1)}, /*in...) while((s32[]{:T(128)}, f32[384,2,128]{2,0,1:T(8,128)}, ...), condition=%wide.region_14.15_spmd.clone, body=%wide.region_10.14_spmd.clone.sunk | while | flops 208517504 | bytes 2972921 | solution.py:131
  258.4 5.0 conditional.10
  313.8 66.6 %while.62 = (s32[]{:T(128)}, f32[384,2,128]{2,0,1:T(8,128)S(1)}, f32[12,512,256]{2,1,0:T(8,128)}, f32[12,512,256]{2,1,0:T(8,128)}, s32[12]{0:T(128)S(1)}, /*inde...) while((s32[]{:T(128)}, f32[384,2,128]{2,0,1:T(8,128)S(1)}, ...), condition=%wide.region_20.21_spmd.clone, body=%wide.region_16.20_spmd.clone.sunk | while | flops 512473984 | bytes 14576473 | solution.py:164
  382.0 15.7 %all-to-all-start.5 = ((bf16[16,24,256]{2,1,0:T(8,128)(2,1)}), bf16[16,24,256]{2,1,0:T(8,128)(2,1)S(1)}, u32[]{:S(2)}, u32[]{:S(2)}) async-start(bf16[16,24,256]{2,1,0:T(8,128)(2,1)} %all_to_all.107), calls=%async_computation.5 | async-start | bytes 393216 | tf_op jit(solution)/shard_map/all_to_all | solution.py:177
  398.5 7.4 %all-to-all-done.5 = bf16[16,24,256]{2,1,0:T(8,128)(2,1)S(1)} async-done(((bf16[16,24,256]{2,1,0:T(8,128)(2,1)}), bf16[16,24,256]{2,1,0:T(8,128)(2,1)S(1)}, u32[]{:S(2)}, u32[]{:S(2)}) %all-to-all-start.5) | async-done | bytes 196640 | tf_op jit(solution)/shard_map/all_to_all | solution.py:177
  410.0 138.8 %reduce-scatter.3.cloned.1.call-done = f32[384,256]{1,0:T(8,128)} async-done(((f32[6144,256]{1,0:T(8,128)}), f32[384,256]{1,0:T(8,128)}) %reduce-scatter.3.cloned.1.call-update) | async-done | bytes 393232 | tf_op jit(solution)/shard_map/reduce_scatter | solution.py:169
  550.5 15.6 %all-to-all-start.6 = ((bf16[16,24,256]{2,1,0:T(8,128)(2,1)}), bf16[16,24,256]{2,1,0:T(8,128)(2,1)S(1)}, u32[]{:S(2)}, u32[]{:S(2)}) async-start(bf16[16,24,256]{2,1,0:T(8,128)(2,1)} %bitcast.30), calls=%async_computation.7 | async-start | bytes 393216 | tf_op jit(solution)/shard_map/all_to_all | solution.py:178
  566.0 68.7 %reduce-scatter.5.cloned.1.call-done = f32[384,256]{1,0:T(8,128)} async-done(((f32[6144,256]{1,0:T(8,128)}), f32[384,256]{1,0:T(8,128)}) %reduce-scatter.5.cloned.1.call-update) | async-done | bytes 393232 | tf_op jit(solution)/shard_map/reduce_scatter | solution.py:170
  636.4 15.5 %all-to-all-start.7 = ((bf16[16,24,256]{2,1,0:T(8,128)(2,1)}), bf16[16,24,256]{2,1,0:T(8,128)(2,1)S(1)}, u32[]{:S(2)}, u32[]{:S(2)}) async-start(bf16[16,24,256]{2,1,0:T(8,128)(2,1)} %bitcast.33), calls=%async_computation.9 | async-start | bytes 393216 | tf_op jit(solution)/shard_map/all_to_all | solution.py:179
  654.0 6.1 all-to-all-done.7
  (363 shorter events, 168.7 us)
Async XLA Ops:
  21.0 8.6 %copy-start.4 = (bf16[24,4,4096]{2,1,0:T(4,128)(2,1)S(1)}, bf16[24,4,4096]{2,1,0:T(4,128)(2,1)}, u32[]{:S(2)}) copy-start(bf16[24,4,4096]{2,1,0:T(4,128)(2,1)} %param.18) | copy-start | bytes 2359300
  21.0 23.0 %all-to-all-start = ((bf16[16,2,12288]{2,1,0:T(2,128)(2,1)}), bf16[16,2,12288]{2,1,0:T(2,128)(2,1)S(1)}, u32[]{:S(2)}, u32[]{:S(2)}) async-start(bf16[16,2,12288]{2,1,0:T(2,128)(2,1)} %reshape.441), calls=%async_computation | async-start | bytes 1572864 | tf_op jit(solution)/shard_map/all_to_all | solution.py:57
  41.6 7.4 %copy-start.5 = (bf16[24,4,4096]{2,1,0:T(4,128)(2,1)S(1)}, bf16[24,4,4096]{2,1,0:T(4,128)(2,1)}, u32[]{:S(2)}) copy-start(bf16[24,4,4096]{2,1,0:T(4,128)(2,1)} %param.20) | copy-start | bytes 2359300
  43.9 19.4 %all-to-all-start.1 = ((bf16[16,2,12288]{2,1,0:T(2,128)(2,1)}), bf16[16,2,12288]{2,1,0:T(2,128)(2,1)S(1)}, u32[]{:S(2)}, u32[]{:S(2)}) async-start(bf16[16,2,12288]{2,1,0:T(2,128)(2,1)} %reshape.439), calls=%async_computation.1 | async-start | bytes 1572864 | tf_op jit(solution)/shard_map/all_to_all | solution.py:56
  61.0 7.6 %copy-start.9 = (s32[32]{0:T(128)S(1)}, s32[32]{0:T(128)}, u32[]{:S(2)}) copy-start(s32[32]{0:T(128)} %param.22) | copy-start | bytes 388
  63.4 28.9 %all-to-all-start.2 = ((bf16[16,2,12288]{2,1,0:T(2,128)(2,1)}), bf16[16,2,12288]{2,1,0:T(2,128)(2,1)S(1)}, u32[]{:S(2)}, u32[]{:S(2)}) async-start(bf16[16,2,12288]{2,1,0:T(2,128)(2,1)} %reshape.437), calls=%async_computation.2 | async-start | bytes 1572864 | tf_op jit(solution)/shard_map/all_to_all | solution.py:58
  68.4 105.6 %all-gather.3.cloned.1.call-start = ((), (), s32[]{:S(2)}) async-start(), calls=%async_computation.10 | async-start | bytes 3342336 | tf_op jit(solution)/shard_map/all_gather | solution.py:72
  103.9 1.4 copy-start.7
  131.2 10.2 %copy-start.8 = (s32[12,12]{1,0:T(8,128)S(1)}, s32[12,12]{1,0:T(8,128)}, u32[]{:S(2)}) copy-start(s32[12,12]{1,0:T(8,128)} %param.23) | copy-start | bytes 1732
  133.3 18.6 %all-to-all-start.4 = ((bf16[16,2,3072]{2,1,0:T(2,128)(2,1)}), bf16[16,2,3072]{2,1,0:T(2,128)(2,1)S(1)}, u32[]{:S(2)}, u32[]{:S(2)}) async-start(bf16[16,2,3072]{2,1,0:T(2,128)(2,1)} %reshape.443), calls=%async_computation.4 | async-start | bytes 393216 | tf_op jit(solution)/shard_map/all_to_all | solution.py:59
  140.5 108.1 %all-gather.5.cloned.1.call-start = ((), (), s32[]{:S(2)}) async-start(), calls=%async_computation.11 | async-start | bytes 3342336 | tf_op jit(solution)/shard_map/all_gather | solution.py:73
  141.3 407.4 %reduce-scatter.3.cloned.1.call-start = ((), (), s32[]{:S(2)}) async-start(), calls=%async_computation.12 | async-start | bytes 6684672 | tf_op jit(solution)/shard_map/reduce_scatter | solution.py:169
  223.4 30.7 %copy-start.1 = (bf16[384,2,128]{2,0,1:T(8,128)(2,1)S(1)}, bf16[384,2,128]{2,0,1:T(8,128)(2,1)}, u32[]{:S(2)}) copy-start(bf16[384,2,128]{2,0,1:T(8,128)(2,1)} %get-tuple-element.1752) | copy-start | bytes 589828
  310.8 2.8 copy-start
  313.8 3.0 copy-start.2
  322.6 3.0 copy-start.2
  327.9 3.0 copy-start.2
  333.1 3.0 copy-start.2
  338.4 3.0 copy-start.2
  343.7 3.0 copy-start.2
  348.9 3.0 copy-start.2
  354.1 3.0 copy-start.2
  359.4 3.0 copy-start.2
  364.6 3.0 copy-start.2
  369.8 3.0 copy-start.2
  375.1 3.0 copy-start.2
  380.4 254.4 %reduce-scatter.5.cloned.1.call-start = ((), (), s32[]{:S(2)}) async-start(), calls=%async_computation.13 | async-start | bytes 6684672 | tf_op jit(solution)/shard_map/reduce_scatter | solution.py:170
  380.9 16.8 %copy-start.6 = (bf16[384,2,128]{2,1,0:T(2,128)(2,1)S(1)}, bf16[384,2,128]{2,1,0:T(2,128)(2,1)}, u32[]{:S(2)}) copy-start(bf16[384,2,128]{2,1,0:T(2,128)(2,1)} %get-tuple-element.1389) | copy-start | bytes 589828
  382.0 23.9 %all-to-all-start.5 = ((bf16[16,24,256]{2,1,0:T(8,128)(2,1)}), bf16[16,24,256]{2,1,0:T(8,128)(2,1)S(1)}, u32[]{:S(2)}, u32[]{:S(2)}) async-start(bf16[16,24,256]{2,1,0:T(8,128)(2,1)} %all_to_all.107), calls=%async_computation.5 | async-start | bytes 393216 | tf_op jit(solution)/shard_map/all_to_all | solution.py:177
  405.9 144.6 %all-to-all-start.3 = ((bf16[16,24,256]{2,1,0:T(8,128)(2,1)}), bf16[16,24,256]{2,1,0:T(8,128)(2,1)S(1)}, u32[]{:S(2)}, u32[]{:S(2)}) async-start(bf16[16,24,256]{2,1,0:T(8,128)(2,1)} %all_to_all.100), calls=%async_computation.3 | async-start | bytes 393216 | tf_op jit(solution)/shard_map/all_to_all | solution.py:176
  550.5 86.0 %all-to-all-start.6 = ((bf16[16,24,256]{2,1,0:T(8,128)(2,1)}), bf16[16,24,256]{2,1,0:T(8,128)(2,1)S(1)}, u32[]{:S(2)}, u32[]{:S(2)}) async-start(bf16[16,24,256]{2,1,0:T(8,128)(2,1)} %bitcast.30), calls=%async_computation.7 | async-start | bytes 393216 | tf_op jit(solution)/shard_map/all_to_all | solution.py:178
  636.4 23.7 %all-to-all-start.7 = ((bf16[16,24,256]{2,1,0:T(8,128)(2,1)}), bf16[16,24,256]{2,1,0:T(8,128)(2,1)S(1)}, u32[]{:S(2)}, u32[]{:S(2)}) async-start(bf16[16,24,256]{2,1,0:T(8,128)(2,1)} %bitcast.33), calls=%async_computation.9 | async-start | bytes 393216 | tf_op jit(solution)/shard_map/all_to_all | solution.py:179
  (1 other events, 0.7 us)
Sparse Core Ops, SparseCore 0:
  105.4 68.4 all-gather.2
  176.3 72.2 all-gather.4
  380.5 168.2 reduce-scatter.2
  551.2 83.5 reduce-scatter.4
where the time goes:
time: 672 us; the launch traced here: 667 us
  waiting for transfers between devices  276 us (41%)
  local copies, waits for them, and re-layouts  144 us (21%)
  matrix products  77.3 us (12%)
  starting transfers between devices  77 us (11%)
  loops' own time  48.9 us (7%)
  other arithmetic  30.4 us (5%)
  between operations  14.1 us (2%)
    reduce_scatter x1, waiting for transfers between devices, on_device(): lax.psum_scatter(key_whole, 'ctx', scatter_dimension=0, tiled=True)  139 us
    unnamed x37, local copies, waits for them, and re-layouts  74.4 us
    dot_general x36, matrix products, block_allow(): jnp.dot(jnp.dot(query_hot, block_mask.astype(jnp.float32)), key_hot.T) > 0.5  69.8 us
    reduce_scatter x1, waiting for transfers between devices, on_device(): lax.psum_scatter(value_whole, 'ctx', scatter_dimension=0, tiled=True)  68.7 us
    all_gather x1, waiting for transfers between devices, on_device(): lax.all_gather(value_loc, 'ctx', axis=0, tiled=True)  25.2 us
    unnamed x1, other arithmetic  22.6 us
    dynamic_slice x36, local copies, waits for them, and re-layouts, on_device(): lax.scan(stats_step, (start_max, start_sum), block_steps)  21.1 us
    dynamic_update_slice x36, local copies, waits for them, and re-layouts, on_device(): lax.scan(backward_step, zero_heads, block_steps)  17.5 us
  transfers between devices with their start and end apart: 12, of which 9 were waited for; matrix products, arithmetic and copies ran while one was open for 18% of the time, Pallas kernels for 0%

commit v1 on v0

v1 whole, which is shorter than its diff:
```python
import jax, jax.numpy as jnp
from jax.sharding import PartitionSpec as P
from jax import lax
from jax.experimental import pallas as pl
from jax.experimental.pallas import tpu as pltpu
BF=jnp.bfloat16; F32=jnp.float32
NB=12; BLK=512; TQ=256; HD=128
SCALE=HD**-0.5
C2=SCALE*1.4426950408889634

def dot(a,b):
    return jnp.dot(a,b,preferred_element_type=F32)

def attend_kernel(where_ref, mask_ref, kv_hbm, qg_ref, dkv_hbm, og_ref,
                  k_vm, v_vm, kt, vt, p_sc, m_sc, dk_acc, dv_acc, ot_acc, dqt_acc, live, sem):
    grp=where_ref[0]; core=where_ref[1]
    loads=[pltpu.make_async_copy(kv_hbm.at[:,i],r.reshape(256,3,8,HD),sem.at[i]) for i,r in enumerate((k_vm,v_vm))]
    for l in loads: l.start()
    @pl.loop(0,NB)
    def _(j):
        z=jnp.zeros((BLK,HD),F32)
        rows=pl.ds(pl.multiple_of(j*BLK,BLK),BLK)
        dk_acc[rows]=z; dv_acc[rows]=z
    for l in loads: l.wait()
    def blk(ref,j):
        return ref[pl.ds(pl.multiple_of(j*64,64),64)].reshape(BLK,HD)
    @pl.loop(0,NB)
    def _(j):
        kt[j]=blk(k_vm,j).T
        vt[j]=blk(v_vm,j).T
    def tile(t,_):
        bm=grp
        b=t*4+bm+(t%2)*(3-2*bm)
        half=(core+t)%2
        q=qg_ref[t,0].reshape(TQ,HD); g=qg_ref[t,1].reshape(TQ,HD)
        qt=q.T; gt=g.T
        def count(j,n):
            live[n]=j
            return n+mask_ref[b,j]
        n_live=lax.fori_loop(0,b,count,0)
        def fwd(j,slot,diag,m,l):
            s=dot(blk(k_vm,j),qt)
            if diag:
                kr=lax.broadcasted_iota(jnp.int32,(BLK,TQ),0); qc=lax.broadcasted_iota(jnp.int32,(BLK,TQ),1)+half*TQ
                s=jnp.where(kr<=qc,s,-1e30)
            m_new=jnp.maximum(m,jnp.max(s,axis=0,keepdims=True))
            mc=m_new*C2
            p=jnp.exp2(s*C2-mc)
            alpha=jnp.exp2(m*C2-mc)
            pb=p.astype(BF)
            p_sc[slot]=pb
            m_sc[slot]=m_new
            l=l*alpha+jnp.sum(p,axis=0,keepdims=True)
            ot_acc[...]=ot_acc[...]*alpha+dot(vt[j],pb)
            return m_new,l
        ot_acc[...]=jnp.zeros((HD,TQ),F32)
        m=jnp.full((1,TQ),-1e30,F32); l=jnp.zeros((1,TQ),F32)
        m,l=fwd(b,NB-1,True,m,l)
        m,l=lax.fori_loop(0,n_live,lambda i,c:fwd(live[i],i,False,*c),(m,l))
        inv=1.0/l
        ot=(ot_acc[...]*inv).astype(BF)
        og_ref[t,0]=ot.T.reshape(32,8,HD)
        r=jnp.sum(gt.astype(F32)*ot.astype(F32),axis=0,keepdims=True)
        mc=m*C2
        def bwd(j,slot,acc):
            f=jnp.exp2(m_sc[slot]*C2-mc)*inv
            p=p_sc[slot].astype(F32)*f
            dp=dot(blk(v_vm,j),gt)
            ds=(p*(dp-r)).astype(BF)
            rows=pl.ds(pl.multiple_of(j*BLK,BLK),BLK)
            dv_acc[rows]+=dot(p.astype(BF),g)
            dk_acc[rows]+=dot(ds,q)
            dqt_acc[...]+=dot(kt[j],ds)
        dqt_acc[...]=jnp.zeros((HD,TQ),F32)
        bwd(b,NB-1,None)
        @pl.loop(0,n_live)
        def _(i):
            bwd(live[i],i,None)
        og_ref[t,1]=(dqt_acc[...]*SCALE).astype(BF).T.reshape(32,8,HD)
        return 0
    lax.fori_loop(0,3,tile,0)
    @pl.loop(0,NB)
    def _(j):
        rows=pl.ds(pl.multiple_of(j*BLK,BLK),BLK)
        un=pl.ds(pl.multiple_of(j*64,64),64)
        k_vm[un]=(dk_acc[rows]*SCALE).astype(BF).reshape(64,8,HD)
        v_vm[un]=dv_acc[rows].astype(BF).reshape(64,8,HD)
    outs=[pltpu.make_async_copy(r.reshape(256,3,8,HD),dkv_hbm.at[:,i],sem.at[i]) for i,r in enumerate((k_vm,v_vm))]
    for l in outs: l.start()
    for l in outs: l.wait()

def attend(where,mask,kv,qg):
    return pl.pallas_call(attend_kernel,
        out_shape=(jax.ShapeDtypeStruct((256,2,3,8,HD),BF),jax.ShapeDtypeStruct((3,2,32,8,HD),BF)),
        in_specs=[pl.BlockSpec(memory_space=pltpu.SMEM)]*2+[pl.BlockSpec(memory_space=pl.ANY),pl.BlockSpec(memory_space=pltpu.VMEM)],
        out_specs=(pl.BlockSpec(memory_space=pl.ANY),pl.BlockSpec(memory_space=pltpu.VMEM)),
        scratch_shapes=[pltpu.VMEM((768,8,HD),BF)]*2+[pltpu.VMEM((NB,HD,BLK),BF)]*2+[
            pltpu.VMEM((NB,BLK,TQ),BF),pltpu.VMEM((NB,1,TQ),F32),pltpu.VMEM((NB*BLK,HD),F32),pltpu.VMEM((NB*BLK,HD),F32),
            pltpu.VMEM((HD,TQ),F32),pltpu.VMEM((HD,TQ),F32),pltpu.SMEM((16,),jnp.int32),pltpu.SemaphoreType.DMA((2,))],
        name="attend",
        compiler_params=pltpu.CompilerParams(vmem_limit_bytes=48<<20))(where,mask,kv,qg)

def place():
    ctx=lax.axis_index("ctx"); hd=lax.axis_index("head")
    return ctx//8, ctx%8, hd//8, (hd%8)//2, hd%2

def device(x, z, y, c):
    return ((x%2)*8+z, (x//2)*8+y*2+c)

def owner(tile):
    blk=tile//2; t=blk//4; bm=blk%4
    return bm+(t%2)*(3-2*bm), (tile%2+t)%2, t

def remote(src, dst, send, recv, dev):
    return pltpu.make_async_remote_copy(src_ref=src, dst_ref=dst, send_sem=send, recv_sem=recv,
                                        device_id=dev, device_id_type=pl.DeviceIdType.MESH)

def greet(x, z, y, c):
    barrier=pltpu.get_barrier_semaphore()
    def plane(i,_):
        z2=i//4; y2=i%4
        @pl.when((z2!=z)|(y2!=y))
        def _():
            pl.semaphore_signal(barrier, inc=1, device_id=device(x,z2,y2,c), device_id_type=pl.DeviceIdType.MESH)
        return 0
    lax.fori_loop(0,32,plane,0)
    def group(i,_):
        x2=i//2; c2=i%2
        @pl.when((x2!=x)|(c2!=c))
        def _():
            pl.semaphore_signal(barrier, inc=1, device_id=device(x2,z,y,c2), device_id_type=pl.DeviceIdType.MESH)
        return 0
    lax.fori_loop(0,8,group,0)

def greeted():
    pl.semaphore_wait(pltpu.get_barrier_semaphore(), 38)

ORDER=(0,1,7,2,6,3,5,4)

def gather_kernel(off, q, k, v, g, kv, qg, q_vm, k_vm, v_vm, g_vm, kv_out, qg_out, qg_in,
                  ld, a_send, a_recv, b_send, b_recv, x_send, x_recv, f_send, f_recv, c_send, c_recv, o_send, o_recv):
    x_lo,z,x_hi,y,c=place()
    x=x_hi*2+x_lo
    right=(x+1)%4; left=(x+3)%4; far=(x+2)%4
    loads=[pltpu.make_async_copy(a,b,ld.at[i]) for i,(a,b) in enumerate(((k,k_vm),(v,v_vm),(q,q_vm),(g,g_vm)))]
    for cp in loads: cp.start()
    greet(x,z,y,c)
    row=lax.broadcasted_iota(jnp.int32,(24,96),0); col=lax.broadcasted_iota(jnp.int32,(24,96),1)
    def pick(ref,h,hot):
        cols=pl.ds(pl.multiple_of(h*HD,HD),HD)
        return dot(hot,ref[:,:,cols].reshape(96,HD)).reshape(3,8,HD).astype(BF)
    def hot_of(h):
        return (col==row*4+off[h]).astype(F32).astype(BF)
    mine=z*4+y
    def to_plane(src, dst, send, recv, z2, y2, self_src):
        @pl.when((z2!=z)|(y2!=y))
        def _():
            remote(src,dst,send,recv,device(x,z2,y2,c)).start()
        @pl.when((z2==z)&(y2==y))
        def _():
            pltpu.make_async_copy(src,dst,recv).start()
    def at(ref,x2,z2,c2):
        return ref.at[x2%2,z2,x2//2,:,c2]
    loads[0].wait(); loads[1].wait()
    greeted()
    def send_kv(i,_):
        z2=(z+i//4)%8; y2=(y+i%4)%4; h=z2*4+y2
        hot=hot_of(h)
        kv_out[h,0]=pick(k_vm,h,hot)
        kv_out[h,1]=pick(v_vm,h,hot)
        to_plane(kv_out.at[h], kv.at[x_lo,z,x_hi,y,c], a_send.at[h], a_recv.at[mine], z2, y2, None)
        return 0
    lax.fori_loop(0,32,send_kv,0)
    loads[2].wait(); loads[3].wait()
    def send_qg(i,_):
        z2=(z+i//4)%8; y2=(y+i%4)%4; h=z2*4+y2
        hot=hot_of(h)
        cols=pl.ds(pl.multiple_of(h*HD,HD),HD)
        qg_out[h,0]=pick(q_vm,h,hot)
        qg_out[h,1]=g_vm[:,:,cols]
        to_plane(qg_out.at[h], qg_in.at[mine], b_send.at[h], b_recv.at[mine], z2, y2, None)
        return 0
    lax.fori_loop(0,32,send_qg,0)
    def chunk(ref,x2,z2):
        return at(ref,x2,z2,c)
    def ring(i,_):
        z2=(z+8-i)%8
        def w(j,_):
            s=z2*4+j
            pltpu.make_async_copy(kv_out.at[0],kv_out.at[0],a_recv.at[s]).wait()
            return 0
        lax.fori_loop(0,4,w,0)
        own=chunk(kv,x,z2)
        remote(own,own,x_send.at[0,z2],x_recv.at[0,z2],device(right,z,y,c)).start()
        remote(own,own,x_send.at[1,z2],x_recv.at[1,z2],device(left,z,y,c)).start()
        remote(own,own,c_send.at[x,z2],c_recv.at[x,z2],device(x,z,y,1-c)).start()
        return 0
    lax.fori_loop(0,8,ring,0)
    def halves(i,_):
        z2=(z+8-i)%8
        a=chunk(kv,left,z2); b=chunk(kv,right,z2)
        remote(a,a,x_send.at[0,z2],x_recv.at[0,z2],device(right,z,y,c)).wait_recv()
        ah=a.at[0:2]
        remote(ah,ah,f_send.at[0,z2],f_recv.at[0,z2],device(right,z,y,c)).start()
        remote(a,a,c_send.at[left,z2],c_recv.at[left,z2],device(x,z,y,1-c)).start()
        remote(b,b,x_send.at[1,z2],x_recv.at[1,z2],device(left,z,y,c)).wait_recv()
        bh=b.at[2:4]
        remote(bh,bh,f_send.at[1,z2],f_recv.at[1,z2],device(left,z,y,c)).start()
        remote(b,b,c_send.at[right,z2],c_recv.at[right,z2],device(x,z,y,1-c)).start()
        return 0
    lax.fori_loop(0,8,halves,0)
    def spread(act):
        def one(i,_):
            z2=(z+8-i//4)%8; y2=i%4; s=z2*4+y2
            act(s, ((x_lo*8+z2)*2+x_hi)*8+y2*2+c)
            return 0
        lax.fori_loop(0,32,one,0)
    def hand(s,first,count,unit,sem,op):
        tile=unit//32; u=unit%32
        xo,co,t=owner(tile)
        src=qg_in.at[s,:,pl.ds(first,count)]; dst=qg.at[t,:,pl.ds(u,count)]
        away=(xo!=x)|(co!=c)
        @pl.when(away)
        def _():
            cp=remote(src,dst,sem,o_recv.at[0],device(xo,z,y,co))
            if op=="start": cp.start()
            else: cp.wait_send()
        if op=="start":
            @pl.when((xo==x)&(co==c))
            def _():
                pltpu.make_async_copy(src,dst,o_recv.at[0]).start()
    def hand_piece(op):
        def act(s,piece):
            if op=="start":
                pltpu.make_async_copy(qg_in.at[0],qg_in.at[0],b_recv.at[s]).wait()
            unit=piece*3
            whole=(unit%32)<=29
            @pl.when(whole)
            def _():
                hand(s,0,3,unit,o_send.at[s,0],op)
            @pl.when((unit%32)>29)
            def _():
                for e in range(3):
                    hand(s,e,1,unit+e,o_send.at[s,e],op)
        return act
    spread(hand_piece("start"))
    def last(i,_):
        z2=(z+8-i)%8
        a=chunk(kv,far,z2)
        ah=a.at[0:2]; bh=a.at[2:4]
        remote(ah,ah,f_send.at[0,z2],f_recv.at[0,z2],device(right,z,y,c)).wait_recv()
        remote(bh,bh,f_send.at[1,z2],f_recv.at[1,z2],device(left,z,y,c)).wait_recv()
        remote(a,a,c_send.at[far,z2],c_recv.at[far,z2],device(x,z,y,1-c)).start()
        return 0
    lax.fori_loop(0,8,last,0)
    def sent(i,_):
        @pl.when(i!=mine)
        def _():
            pltpu.make_async_copy(kv_out.at[0],kv_out.at[0],a_send.at[i]).wait()
            pltpu.make_async_copy(qg_out.at[0],qg_out.at[0],b_send.at[i]).wait()
        return 0
    lax.fori_loop(0,32,sent,0)
    spread(hand_piece("done"))
    def ring_sent(z2,_):
        own=chunk(kv,x,z2)
        for d in range(2):
            remote(own,own,x_send.at[d,z2],x_recv.at[d,z2],device(right,z,y,c)).wait_send()
            hf=own.at[2*d:2*d+2]
            remote(hf,hf,f_send.at[d,z2],f_recv.at[d,z2],device(right,z,y,c)).wait_send()
        for x2 in range(4):
            theirs=at(kv,jnp.int32(x2),z2,1-c)
            cp=remote(theirs,theirs,c_send.at[x2,z2],c_recv.at[x2,z2],device(x,z,y,1-c))
            cp.wait_send()
            cp.wait_recv()
        return 0
    lax.fori_loop(0,8,ring_sent,0)
    pltpu.make_async_copy(qg,qg,o_recv.at[0]).wait()

KV=(2,8,2,4,2,2,3,8,HD)
DMA=pltpu.SemaphoreType.DMA
ANY=pl.BlockSpec(memory_space=pl.ANY)
def gather(off,q,k,v,g):
    return pl.pallas_call(gather_kernel,
        out_shape=(jax.ShapeDtypeStruct(KV,BF),jax.ShapeDtypeStruct((3,2,32,8,HD),BF)),
        in_specs=[pl.BlockSpec(memory_space=pltpu.SMEM)]+[ANY]*4,
        out_specs=(ANY,ANY),
        scratch_shapes=[pltpu.VMEM((24,4,4096),BF)]*3+[pltpu.VMEM((3,8,4096),BF)]+[pltpu.VMEM((32,2,3,8,HD),BF)]*3+[
            DMA((4,)),DMA((32,)),DMA((32,)),DMA((32,)),DMA((32,)),DMA((2,8)),DMA((2,8)),DMA((2,8)),DMA((2,8)),DMA((4,8)),DMA((4,8)),DMA((32,3)),DMA((1,))],
        name="gather",
        compiler_params=pltpu.CompilerParams(collective_id=0,has_side_effects=True,vmem_limit_bytes=32<<20))(off,q,k,v,g)

def scatter_kernel(dkv, og, o_out, dq_out, dk_out, dv_out,
                   own, theirs, far_in, near_in, last_in, og_in, fin,
                   ld, c_send, c_recv, g_send, g_recv, far_send, far_recv, near_send, near_recv, last_send, last_recv, p_send, p_recv):
    x_lo,z,x_hi,y,c=place()
    x=x_hi*2+x_lo
    right=(x+1)%4; left=(x+3)%4; far=(x+2)%4
    mine=z*4+y
    cols=pl.ds(pl.multiple_of(mine*HD,HD),HD)
    outs=(o_out,dq_out,dk_out,dv_out)
    def load(z2):
        return pltpu.make_async_copy(dkv.at[:,z2,:,:,c],own.at[:,z2],ld.at[z2])
    def swap(z2):
        return remote(dkv.at[:,z2,:,:,1-c],theirs.at[:,z2],c_send.at[z2],c_recv.at[z2],device(x,z,y,1-c))
    def start_load(i,_):
        load((z+i)%8).start()
        return 0
    greet(x,z,y,c)
    lax.fori_loop(0,8,start_load,0)
    greeted()
    def back(op):
        def one(i,_):
            t=i//12; e=i%12
            blk=t*4+x+(t%2)*(3-2*x)
            tile=2*blk+(c+t)%2
            def hand(unit,count,sem):
                piece=unit//3; k=unit%3; u=unit-tile*32
                xp=((piece//8)%2)*2+(piece//128)
                zp=(piece//16)%8; yp=(piece%8)//2; cp_=piece%2
                s=zp*4+yp
                src=og.at[t,:,pl.ds(u,count)]; dst=og_in.at[s,:,pl.ds(k,count)]
                away=(xp!=x)|(cp_!=c)
                @pl.when(away)
                def _():
                    cp=remote(src,dst,sem,g_recv.at[s],device(xp,z,y,cp_))
                    if op=="start": cp.start()
                    else: cp.wait_send()
                if op=="start":
                    @pl.when((xp==x)&(cp_==c))
                    def _():
                        pltpu.make_async_copy(src,dst,g_recv.at[s]).start()
            @pl.when(e<10)
            def _():
                hand(((tile*32+2)//3+e)*3,3,g_send.at[i])
            @pl.when(e>=10)
            def _():
                n=e-10; r=tile%3
                hand(tile*32+n+30*(1-(r+1)//2)+30*n*(r%2),1,g_send.at[i])
            return 0
        lax.fori_loop(0,36,one,0)
    def start_swap(i,_):
        swap((z+i)%8).start()
        return 0
    lax.fori_loop(0,8,start_swap,0)
    back("start")
    def to_rows(a, src, s):
        z2=s//4; y2=s%4
        dst=outs[a].at[:,:,cols]
        @pl.when(s!=mine)
        def _():
            remote(src,dst,p_send.at[a,s],p_recv.at[a],device(x,z2,y2,c)).start()
        @pl.when(s==mine)
        def _():
            pltpu.make_async_copy(src,dst,p_recv.at[a]).start()
    def sum_cores(i,_):
        z2=(z+i)%8
        load(z2).wait()
        swap(z2).wait_recv()
        for xl in range(2):
            for xh in range(2):
                own[xl,z2,xh]=(own[xl,z2,xh].astype(F32)+theirs[xl,z2,xh].astype(F32)).astype(BF)
        ef=own.at[far%2,z2,far//2]; er=own.at[right%2,z2,right//2]; el=own.at[left%2,z2,left//2]
        remote(ef.at[0:2],far_in.at[0,z2],far_send.at[0,z2],far_recv.at[0,z2],device(right,z,y,c)).start()
        remote(ef.at[2:4],far_in.at[1,z2],far_send.at[1,z2],far_recv.at[1,z2],device(left,z,y,c)).start()
        remote(er.at[2:4],near_in.at[0,z2],near_send.at[0,z2],near_recv.at[0,z2],device(right,z,y,c)).start()
        remote(el.at[0:2],near_in.at[1,z2],near_send.at[1,z2],near_recv.at[1,z2],device(left,z,y,c)).start()
        return 0
    lax.fori_loop(0,8,sum_cores,0)
    def rows_back(i,_):
        s=((z+i//4)%8)*4+(y+i%4)%4
        pltpu.make_async_copy(og_in.at[s],og_in.at[s],g_recv.at[s]).wait()
        to_rows(0,og_in.at[s,0],s)
        to_rows(1,og_in.at[s,1],s)
        return 0
    lax.fori_loop(0,32,rows_back,0)
    def relay(i,_):
        z2=(z+i)%8
        for d,peer in ((0,right),(1,left)):
            lo=2*d
            buf=far_in.at[d,z2]
            pltpu.make_async_copy(buf,buf,far_recv.at[d,z2]).wait()
            far_in[d,z2]=(far_in[d,z2].astype(F32)+own[peer%2,z2,peer//2,lo:lo+2].astype(F32)).astype(BF)
            remote(buf,last_in.at[d,z2],last_send.at[d,z2],last_recv.at[d,z2],device(peer,z,y,c)).start()
        return 0
    lax.fori_loop(0,8,relay,0)
    def finish(i,_):
        z2=(z+i)%8
        for d in range(2):
            pltpu.make_async_copy(last_in.at[d,z2],last_in.at[d,z2],last_recv.at[d,z2]).wait()
            pltpu.make_async_copy(near_in.at[d,z2],near_in.at[d,z2],near_recv.at[d,z2]).wait()
        for d in range(2):
            lo=2*d
            fin[z2,lo:lo+2]=(own[x_lo,z2,x_hi,lo:lo+2].astype(F32)+last_in[d,z2].astype(F32)+near_in[1-d,z2].astype(F32)).astype(BF)
        for j in range(4):
            y2=(y+j)%4
            to_rows(2,fin.at[z2,y2,0],z2*4+y2)
            to_rows(3,fin.at[z2,y2,1],z2*4+y2)
        return 0
    lax.fori_loop(0,8,finish,0)
    back("done")
    def sent(i,_):
        swap(i).wait_send()
        for d in range(2):
            b=far_in.at[d,i]
            for sem in (far_send,near_send,last_send):
                pltpu.make_async_copy(b,b,sem.at[d,i]).wait()
        return 0
    lax.fori_loop(0,8,sent,0)
    def rows_sent(i,_):
        @pl.when(i!=mine)
        def _():
            for a in range(4):
                pltpu.make_async_copy(fin.at[0,0,0],fin.at[0,0,0],p_send.at[a,i]).wait()
        return 0
    lax.fori_loop(0,32,rows_sent,0)
    for a in range(4):
        pltpu.make_async_copy(outs[a],outs[a],p_recv.at[a]).wait()

def scatter(dkv,og):
    return pl.pallas_call(scatter_kernel,
        out_shape=(jax.ShapeDtypeStruct((3,8,4096),BF),)*4,
        in_specs=[ANY]*2,
        out_specs=(ANY,)*4,
        scratch_shapes=[pltpu.VMEM((2,8,2,4,2,3,8,HD),BF)]*2+[pltpu.VMEM((2,8,2,2,3,8,HD),BF)]*3+[pltpu.VMEM((32,2,3,8,HD),BF),pltpu.VMEM((8,4,2,3,8,HD),BF),
            DMA((8,)),DMA((8,)),DMA((8,)),DMA((36,)),DMA((32,))]+[DMA((2,8))]*6+[DMA((4,32)),DMA((4,))],
        name="scatter",
        compiler_params=pltpu.CompilerParams(collective_id=1,has_side_effects=True,vmem_limit_bytes=32<<20))(dkv,og)

def on_device(queries,key_states,value_states,out_grad,offsets,block_mask):
    kv,qg=gather(offsets,queries,key_states,value_states,out_grad.reshape(3,8,4096))
    x_lo,z,x_hi,y,c=place()
    where=jnp.stack([x_hi*2+x_lo,c]).astype(jnp.int32)
    dkv,og=attend(where,block_mask,kv.reshape(256,2,3,8,HD),qg)
    outs=scatter(dkv.reshape(KV),og)
    return tuple(o.reshape(24,4096) for o in outs)


def solution(mesh):
    rows3=P(("ctx","head"),None,None); rows2=P(("ctx","head"),None)
    return jax.shard_map(on_device,mesh=mesh,in_specs=(rows3,rows3,rows3,rows2,P(),P()),
                         out_specs=(rows2,)*4,check_vma=False)
```

time: 672 us -> 108 us (0.16)
  waiting for transfers between devices: 276 us -> 0 us
  local copies, waits for them, and re-layouts: 144 us -> 10 us
  Pallas kernels: 0 us -> 95.4 us
  matrix products: 77.3 us -> 0 us
  starting transfers between devices: 77 us -> 0 us
  loops' own time: 48.9 us -> 0 us
  other arithmetic: 30.4 us -> 0.08 us
  between operations: 14.1 us -> 0.7 us
    reduce_scatter x2 -> x0, waiting for transfers between devices: 207 us -> none  [the longest x1 139 us: on_device(): lax.psum_scatter(key_whole, 'ctx', scatter_dimension=0, tiled=True)]
    pallas_call x0 -> x3, Pallas kernels: none -> 95.4 us  [the longest x1 44 us: gather(): pl.pallas_call(gather_kernel, out_shape=(jax.ShapeDtypeStruct(KV, BF), ja...]
    dot_general x44 -> x0, matrix products: 77.3 us -> none  [the longest x36 69.8 us: block_allow(): jnp.dot(jnp.dot(query_hot, block_mask.astype(jnp.float32)), key_hot.T) > 0.5]
    all_to_all x8 -> x0, starting transfers between devices: 76.7 us -> none  [the longest x1 15.7 us: on_device(): lax.all_to_all(query_grad, 'head', split_axis=0, concat_axis=1, tiled=True)]
    unnamed x37 -> x18, local copies, waits for them, and re-layouts: 74.4 us -> 10 us
    another operation x39 -> x0, loops' own time: 48.9 us -> none  [the longest x1 16.2 us: on_device(): lax.scan(backward_step, zero_heads, block_steps)]
    all_gather x2 -> x0, waiting for transfers between devices: 39.7 us -> none  [the longest x1 25.2 us: on_device(): lax.all_gather(value_loc, 'ctx', axis=0, tiled=True)]
    all_to_all x8 -> x0, waiting for transfers between devices: 27.8 us -> none  [the longest x1 9.61 us: on_device(): lax.all_to_all(out_grad[:, None, :], 'head', split_axis=2, concat_axis=0,...]
  transfers between devices with their start and end apart: 12 -> 0, of which waited for: 9 -> 0; matrix products, arithmetic and copies ran while one was open for 18% -> 0% of each run, Pallas kernels for 0% -> 0%
where the time goes in v1:
time: 108 us; the launch traced here: 106 us
  Pallas kernels  95.4 us (88%)
  local copies, waits for them, and re-layouts  10 us (9%)
    pallas_call x1, Pallas kernels, gather(): pl.pallas_call(gather_kernel, out_shape=(jax.ShapeDtypeStruct(KV, BF), ja...  44 us
    pallas_call x1, Pallas kernels, scatter(): pl.pallas_call(scatter_kernel, out_shape=(jax.ShapeDtypeStruct((3, 8, 409...  35.1 us
    pallas_call x1, Pallas kernels, attend(): pl.pallas_call(attend_kernel, out_shape=(jax.ShapeDtypeStruct((256, 2, 3,...  16.3 us
    unnamed x18, local copies, waits for them, and re-layouts  10 us

profile of v1, /device:TPU:1, one launch (start us, length us, event | category | flops | bytes accessed | tf_op | source)
XLA Modules:
  0.0 106.2 jit_solution(4567983042277795258)
XLA Ops:
  0.7 0.1 pad_add_fusion.where_ref
  0.7 0.0 copy-start.1
  0.7 1.1 %copy-done.1 = bf16[24,4,4096]{2,1,0:T(4,128)(2,1)S(1)} copy-done((bf16[24,4,4096]{2,1,0:T(4,128)(2,1)S(1)}, bf16[24,4,4096]{2,1,0:T(4,128)(2,1)}, u32[]{:S(2)}) %copy-start.1) | copy-done | bytes 786456
  1.9 0.0 copy-start.2
  1.9 1.1 %copy-done.2 = bf16[24,4,4096]{2,1,0:T(4,128)(2,1)S(1)} copy-done((bf16[24,4,4096]{2,1,0:T(4,128)(2,1)S(1)}, bf16[24,4,4096]{2,1,0:T(4,128)(2,1)}, u32[]{:S(2)}) %copy-start.2) | copy-done | bytes 786456
  3.0 0.0 copy-start.3
  3.0 1.1 %copy-done.3 = bf16[24,4,4096]{2,1,0:T(4,128)(2,1)S(1)} copy-done((bf16[24,4,4096]{2,1,0:T(4,128)(2,1)S(1)}, bf16[24,4,4096]{2,1,0:T(4,128)(2,1)}, u32[]{:S(2)}) %copy-start.3) | copy-done | bytes 786456
  4.1 0.0 copy-start.4
  4.1 0.9 copy-done.4
  5.1 0.0 copy-start.6
  5.1 0.7 copy-done.6
  5.7 44.0 %gather.1 = (bf16[2,8,2,4,2,2,3,8,128]{8,7,6,5,4,3,2,1,0:T(8,128)(2,1)S(1)}, bf16[3,2,32,8,128]{4,3,2,1,0:T(8,128)(2,1)S(1)}) custom-call(s32[32]{0:T(128)S(1)} %copy-done.6, bf16[24,4,4096]{2,1,0:T(4,128)(2,1)S(1)} %copy-done.1, bf16[24,4,4096]{2,1,0:T(4,128)(2,1)S(1)} %copy-done.2, bf16[24,4,4096]{2,1,0:T(4,128)(2,1)S(1)} %copy-done.3, ...), custom_call_target="tpu_custom_call" | custom-call | tf_op jit(solution)/shard_map/gather/pallas_call | solution.py:283
  49.7 0.0 copy-start
  49.8 1.6 %copy-done = bf16[2,8,2,4,2,2,3,8,128]{8,7,6,5,4,3,2,1,0:T(8,128)(2,1)} copy-done((bf16[2,8,2,4,2,2,3,8,128]{8,7,6,5,4,3,2,1,0:T(8,128)(2,1)}, bf16[2,8,2,4,2,2,3,8,128]{8,7,6,5,4,3,2,1,0:T(8,128)(2,1)S(1)}, u32[]{:S(2)}) %copy-start) | copy-done | bytes 3145752
  51.4 0.0 copy-start.5
  51.4 0.7 copy-done.5
  52.1 16.3 %attend.1 = (bf16[256,2,3,8,128]{4,3,2,1,0:T(8,128)(2,1)S(1)}, bf16[3,2,32,8,128]{4,3,2,1,0:T(8,128)(2,1)S(1)}) custom-call(s32[2]{0:T(128)S(1)} %pad_add_fusion.where_ref, s32[12,12]{1,0:T(8,128)S(1)} %copy-done.5, bf16[256,2,3,8,128]{4,3,2,1,0:T(8,128)(2,1)} %bitcast.10, bf16[3,2,32,8,128]{4,3,2,1,0:T(8,128)(2,1)S(1)} %get-tuple-element.13.qg_ref), custom_call_target="tpu_custom_call" | custom-call | tf_op jit(solution)/shard_map/attend/pallas_call | solution.py:93
  68.4 35.1 %scatter.1 = (bf16[3,8,4096]{2,1,0:T(8,128)(2,1)S(1)}, bf16[3,8,4096]{2,1,0:T(8,128)(2,1)S(1)}, bf16[3,8,4096]{2,1,0:T(8,128)(2,1)S(1)}, bf16[3,8,4096]{2,1,0:T(8,128)(2,1)S(1)}) custom-call(bf16[2,8,2,4,2,2,3,8,128]{8,7,6,5,4,3,2,1,0:T(8,128)(2,1)S(1)} %bitcast.9, bf16[3,2,32,8,128]{4,3,2,1,0:T(8,128)(2,1)S(1)} %get-tuple-element.15.og), custom_call_target="tpu_custom_call" | custom-call | tf_op jit(solution)/shard_map/scatter/pallas_call | solution.py:420
  103.5 0.7 copy.14
  104.2 0.7 copy.15
  104.8 0.7 copy.16
  105.5 0.7 copy.17
Async XLA Ops:
  0.7 1.1 %copy-start.1 = (bf16[24,4,4096]{2,1,0:T(4,128)(2,1)S(1)}, bf16[24,4,4096]{2,1,0:T(4,128)(2,1)}, u32[]{:S(2)}) copy-start(bf16[24,4,4096]{2,1,0:T(4,128)(2,1)} %q.1) | copy-start | bytes 2359300
  1.9 1.1 %copy-start.2 = (bf16[24,4,4096]{2,1,0:T(4,128)(2,1)S(1)}, bf16[24,4,4096]{2,1,0:T(4,128)(2,1)}, u32[]{:S(2)}) copy-start(bf16[24,4,4096]{2,1,0:T(4,128)(2,1)} %k.1) | copy-start | bytes 2359300
  3.0 1.1 %copy-start.3 = (bf16[24,4,4096]{2,1,0:T(4,128)(2,1)S(1)}, bf16[24,4,4096]{2,1,0:T(4,128)(2,1)}, u32[]{:S(2)}) copy-start(bf16[24,4,4096]{2,1,0:T(4,128)(2,1)} %v.1) | copy-start | bytes 2359300
  4.1 0.9 copy-start.4
  5.1 0.7 copy-start.6
  49.7 1.6 %copy-start = (bf16[2,8,2,4,2,2,3,8,128]{8,7,6,5,4,3,2,1,0:T(8,128)(2,1)}, bf16[2,8,2,4,2,2,3,8,128]{8,7,6,5,4,3,2,1,0:T(8,128)(2,1)S(1)}, u32[]{:S(2)}) copy-start(bf16[2,8,2,4,2,2,3,8,128]{8,7,6,5,4,3,2,1,0:T(8,128)(2,1)S(1)} %get-tuple-element.12) | copy-start | bytes 9437188
  51.4 0.7 copy-start.5

commit v2 on v1

v2 whole, which is shorter than its diff:
```python
import functools, jax, jax.numpy as jnp
from jax.sharding import PartitionSpec as P
from jax import lax
from jax.experimental import pallas as pl
from jax.experimental.pallas import tpu as pltpu
BF=jnp.bfloat16; F32=jnp.float32
HEADS=32; NB=12; BLK=512; TQ=256; HD=128
SCALE=HD**-0.5
C2=SCALE*1.4426950408889634
GF=2; GB=2

def dot(a,b):
    return jnp.dot(a,b,preferred_element_type=F32)

def dot_t(a,b):
    return lax.dot_general(a,b,(((0,),(0,)),((),())),preferred_element_type=F32)

def my_tiles():
    ctx=lax.axis_index("ctx"); hd=lax.axis_index("head")
    return (hd//8)*2+ctx//8, hd%2

def attend_kernel(mask_hbm, kv_ref, qg_ref, dkv_ref, og_ref,
                  p_sc, m_sc, dk_acc, dv_acc, ot_acc, dqt_acc, live, mask_ref, ld):
    grp,core=my_tiles()
    fetch=pltpu.make_async_copy(mask_hbm,mask_ref,ld.at[0])
    fetch.start()
    kv_rows=kv_ref.reshape(2,768,8,HD)
    dkv_rows=dkv_ref.reshape(2,768,8,HD)
    def blk(i,j):
        return kv_rows[i,pl.ds(pl.multiple_of(j*64,64),64)].reshape(BLK,HD)
    @pl.loop(0,NB)
    def _(j):
        z=jnp.zeros((BLK,HD),F32)
        rows=pl.ds(pl.multiple_of(j*BLK,BLK),BLK)
        dk_acc[rows]=z; dv_acc[rows]=z
    def tile(t):
        bm=grp
        b=t*4+bm+(t%2)*(3-2*bm)
        half=(core+t)%2
        q=qg_ref[t,0].reshape(TQ,HD); g=qg_ref[t,1].reshape(TQ,HD)
        qt=q.T; gt=g.T
        def count(j,n):
            live[n]=j
            return n+mask_ref[b,j]
        n_live=lax.fori_loop(0,b,count,0)
        def fwd(js,slots,diag,m,l):
            ss=[]
            for j in js:
                s=dot(blk(0,j),qt)
                if diag:
                    kr=lax.broadcasted_iota(jnp.int32,(BLK,TQ),0); qc=lax.broadcasted_iota(jnp.int32,(BLK,TQ),1)+half*TQ
                    s=jnp.where(kr<=qc,s,-1e30)
                ss.append(s)
            m_new=m
            for s in ss: m_new=jnp.maximum(m_new,jnp.max(s,axis=0,keepdims=True))
            mc=m_new*C2
            alpha=jnp.exp2(m*C2-mc)
            l=l*alpha
            acc=ot_acc[...]*alpha
            for j,slot,s in zip(js,slots,ss):
                p=jnp.exp2(s*C2-mc)
                pb=p.astype(BF)
                p_sc[slot]=pb
                m_sc[slot]=m_new
                l=l+jnp.sum(p,axis=0,keepdims=True)
                acc=acc+dot_t(blk(1,j),pb)
            ot_acc[...]=acc
            return m_new,l
        def run(group,step,carry):
            whole=n_live//group
            def body(i,c):
                idx=[i*group+e for e in range(group)]
                return step([live[e] for e in idx],idx,c)
            carry=lax.fori_loop(0,whole,body,carry)
            if group>1:
                carry=lax.fori_loop(whole*group,n_live,lambda i,c: step([live[i]],[i],c),carry)
            return carry
        ot_acc[...]=jnp.zeros((HD,TQ),F32)
        m=jnp.full((1,TQ),-1e30,F32); l=jnp.zeros((1,TQ),F32)
        m,l=fwd([b],[NB-1],True,m,l)
        m,l=run(GF,lambda js,sl,c: fwd(js,sl,False,*c),(m,l))
        inv=1.0/l
        ot=(ot_acc[...]*inv).astype(BF)
        og_ref[t,0]=ot.T.reshape(32,8,HD)
        r=jnp.sum(gt.astype(F32)*ot.astype(F32),axis=0,keepdims=True)
        mc=m*C2
        def bwd(js,slots,c):
            acc=dqt_acc[...]
            for j,slot in zip(js,slots):
                f=jnp.exp2(m_sc[slot]*C2-mc)*inv
                p=p_sc[slot].astype(F32)*f
                dp=dot(blk(1,j),gt)
                ds=(p*(dp-r)).astype(BF)
                rows=pl.ds(pl.multiple_of(j*BLK,BLK),BLK)
                dv_acc[rows]+=dot(p.astype(BF),g)
                dk_acc[rows]+=dot(ds,q)
                acc=acc+dot_t(blk(0,j),ds)
            dqt_acc[...]=acc
            return c
        dqt_acc[...]=jnp.zeros((HD,TQ),F32)
        bwd([b],[NB-1],0)
        run(GB,bwd,0)
        og_ref[t,1]=(dqt_acc[...]*SCALE).astype(BF).T.reshape(32,8,HD)
    def settle_blocks(lo,hi):
        @pl.loop(lo,hi)
        def _(j):
            rows=pl.ds(pl.multiple_of(j*BLK,BLK),BLK)
            un=pl.ds(pl.multiple_of(j*64,64),64)
            dkv_rows[0,un]=(dk_acc[rows]*SCALE).astype(BF).reshape(64,8,HD)
            dkv_rows[1,un]=dv_acc[rows].astype(BF).reshape(64,8,HD)
    fetch.wait()
    @pl.loop(0,3)
    def _(t):
        tile(t)
    settle_blocks(0,NB)

KV=(2,2,8,2,4,2,3,8,HD)
QG=(3,2,32,8,HD)
VM=pl.BlockSpec(memory_space=pltpu.VMEM)
ANY=pl.BlockSpec(memory_space=pl.ANY)
DMA=pltpu.SemaphoreType.DMA
def held(x):
    return pltpu.with_memory_space_constraint(x,pltpu.VMEM)
def afar(x):
    return pltpu.with_memory_space_constraint(x,pltpu.HBM)
def attend(mask,kv,qg):
    return pl.pallas_call(attend_kernel,
        out_shape=(pltpu.VMEM(KV,BF),pltpu.VMEM(QG,BF)),
        in_specs=[ANY,VM,VM],
        out_specs=(VM,VM),
        scratch_shapes=[
            pltpu.VMEM((NB,BLK,TQ),BF),pltpu.VMEM((NB,1,TQ),F32),pltpu.VMEM((NB*BLK,HD),F32),pltpu.VMEM((NB*BLK,HD),F32),
            pltpu.VMEM((HD,TQ),F32),pltpu.VMEM((HD,TQ),F32),pltpu.SMEM((16,),jnp.int32),pltpu.SMEM((NB,NB),jnp.int32),DMA((1,))],
        name="attend",
        compiler_params=pltpu.CompilerParams(vmem_limit_bytes=40<<20))(afar(mask),held(kv),held(qg))

MESH=pl.DeviceIdType.MESH

def place():
    ctx=lax.axis_index("ctx"); hd=lax.axis_index("head")
    return ctx//8, ctx%8, hd//8, (hd%8)//2, hd%2

def device(x, z, y, c):
    return ((x%2)*8+z, (x//2)*8+y*2+c)

def owner(tile):
    blk=tile//2; t=blk//4; bm=blk%4
    return bm+(t%2)*(3-2*bm), (tile%2+t)%2, t

def order(i):
    return (i%2)*((i+1)//2)+(1-i%2)*((8-i//2)%8)

def remote(src, dst, send, recv, dev):
    return pltpu.make_async_remote_copy(src_ref=src, dst_ref=dst, send_sem=send, recv_sem=recv,
                                        device_id=dev, device_id_type=MESH)

def wait_for(ref, sem):
    pltpu.make_async_copy(ref,ref,sem).wait()

def greet(x, z, y, c):
    barrier=pltpu.get_barrier_semaphore()
    def plane(i,_):
        s=(z*4+y+i)%32
        pl.semaphore_signal(barrier, inc=1, device_id=device(x,s//4,s%4,c), device_id_type=MESH)
        return 0
    lax.fori_loop(1,32,plane,0,unroll=True)
    for i in range(1,8):
        s=(x*2+c+i)%8
        pl.semaphore_signal(barrier, inc=1, device_id=device(s//2,z,y,s%2), device_id_type=MESH)

def greeted():
    pl.semaphore_wait(pltpu.get_barrier_semaphore(), 38)

def gather_kernel(off_hbm, q, k, v, g, kv, qg, q_vm, k_vm, v_vm, g_vm, kv_out, qg_out, qg_in,
                  off, ld, a_send, a_recv, b_send, b_recv, x_send, x_recv, f_send, f_recv, c_send, c_recv, o_send, o_recv):
    x_lo,z,x_hi,y,c=place()
    x=x_hi*2+x_lo
    right=(x+1)%4; left=(x+3)%4; far=(x+2)%4
    mine=z*4+y
    for i in range(8):
        cols=pl.ds(pl.multiple_of(((z+order(i))%8)*512,512),512)
        pltpu.make_async_copy(k.at[:,:,cols],k_vm.at[:,:,cols],ld.at[i]).start()
        pltpu.make_async_copy(v.at[:,:,cols],v_vm.at[:,:,cols],ld.at[i]).start()
    pltpu.make_async_copy(q,q_vm,ld.at[8]).start()
    pltpu.make_async_copy(g,g_vm,ld.at[9]).start()
    fetch=pltpu.make_async_copy(off_hbm,off,ld.at[10])
    fetch.start()
    greet(x,z,y,c)
    row=lax.broadcasted_iota(jnp.int32,(24,96),0); col=lax.broadcasted_iota(jnp.int32,(24,96),1)
    lead=col-row*4
    def columns(h):
        return pl.ds(pl.multiple_of(h*HD,HD),HD)
    def pick(ref,h,hot):
        return dot(hot,ref[:,:,columns(h)].reshape(96,HD)).reshape(3,8,HD).astype(BF)
    def hot_of(h):
        return (lead==off[h]).astype(F32).astype(BF)
    def chunk(x2,z2):
        return kv.at[:,x2%2,z2,x2//2,:,c]
    def pick_kv(i):
        wait_for(k_vm.at[:,:,pl.ds(0,1024)],ld.at[i])
        z2=(z+order(i))%8
        for j in range(4):
            h=z2*4+(y+j)%4
            hot=hot_of(h)
            kv_out[h,0]=pick(k_vm,h,hot)
            kv_out[h,1]=pick(v_vm,h,hot)
    def pick_qg(i):
        z2=(z+order(i))%8
        for j in range(4):
            h=z2*4+(y+j)%4
            qg_out[h,0]=pick(q_vm,h,hot_of(h))
            qg_out[h,1]=g_vm[:,:,columns(h)]
    def to_plane(i, out, dst, send, recv):
        z2=(z+order(i))%8
        for j in range(4):
            y2=(y+j)%4
            src=out.at[z2*4+y2]
            if isinstance(i,int) and i==0 and j==0:
                pltpu.make_async_copy(src,dst,recv).start()
            else:
                remote(src,dst,send,recv,device(x,z2,y2,c)).start()
    def send_kv(i):
        to_plane(i,kv_out,kv.at[:,x_lo,z,x_hi,y,c],a_send.at[0],a_recv.at[i])
    def send_qg(i):
        to_plane(i,qg_out,qg_in.at[mine],b_send.at[0],b_recv.at[i])
    def ring(i):
        z2=(z+8-order(i))%8
        wait_for(kv_out.at[0:4],a_recv.at[i])
        own=chunk(x,z2)
        remote(own,own,x_send.at[0],x_recv.at[0,i],device(right,z,y,c)).start()
        remote(own,own,x_send.at[1],x_recv.at[1,i],device(left,z,y,c)).start()
        remote(own,own,c_send.at[0],c_recv.at[0],device(x,z,y,1-c)).start()
    def halves(i):
        z2=(z+8-order(i))%8
        for d,frm,to in ((0,left,right),(1,right,left)):
            a=chunk(frm,z2)
            wait_for(a,x_recv.at[d,i])
            ah=a.at[:,2*d:2*d+2]
            remote(ah,ah,f_send.at[d],f_recv.at[i],device(to,z,y,c)).start()
            remote(a,a,c_send.at[0],c_recv.at[0],device(x,z,y,1-c)).start()
    def last(i):
        z2=(z+8-order(i))%8
        a=chunk(far,z2)
        wait_for(a,f_recv.at[i])
        remote(a,a,c_send.at[0],c_recv.at[0],device(x,z,y,1-c)).start()
    def hand(s,first,count,unit,op):
        tile=unit//32; u=unit%32
        xo,co,t=owner(tile)
        src=qg_in.at[s,:,pl.ds(first,count)]; dst=qg.at[t,:,pl.ds(u,count)]
        @pl.when((xo!=x)|(co!=c))
        def _():
            cp=remote(src,dst,o_send.at[0],o_recv.at[0],device(xo,z,y,co))
            if op=="start": cp.start()
            else: cp.wait_send()
        if op=="start":
            @pl.when((xo==x)&(co==c))
            def _():
                pltpu.make_async_copy(src,dst,o_recv.at[0]).start()
    def spread(i,op):
        z2=(z+8-order(i))%8
        if op=="start":
            wait_for(qg_in.at[0:4],b_recv.at[i])
        def one(y2,_):
            s=z2*4+y2
            unit=(((x_lo*8+z2)*2+x_hi)*8+y2*2+c)*3
            @pl.when((unit%32)<=29)
            def _():
                hand(s,0,3,unit,op)
            @pl.when((unit%32)>29)
            def _():
                for e in range(3):
                    hand(s,e,1,unit+e,op)
            return 0
        lax.fori_loop(0,4,one,0)
    def loop(lo,hi,*acts):
        def body(i,_):
            for act in acts: act(i)
            return 0
        lax.fori_loop(lo,hi,body,0)
    def seq(lo,hi,*acts):
        loop(lo,hi,*[(lambda i,f=f,d=d: f(i+d)) for f,d in acts])
    def spread_start(i):
        spread(i,"start")
    fetch.wait()
    pick_kv(0)
    greeted()
    send_kv(0)
    loop(1,8,pick_kv,send_kv)
    wait_for(q_vm,ld.at[8]); wait_for(g_vm,ld.at[9])
    pick_qg(0); send_qg(0); ring(0)
    loop(1,8,pick_qg,send_qg,ring)
    loop(0,4,halves)
    seq(4,8,(halves,0),(spread_start,-4))
    seq(0,4,(last,0),(spread_start,4))
    loop(4,8,last)
    wait_for(kv_out.at[0:31],a_send.at[0])
    wait_for(qg_out.at[0:31],b_send.at[0])
    loop(0,8,lambda i: spread(i,"done"))
    for d in range(2):
        wait_for(kv.at[:,0,:,0,:,0],x_send.at[d])
        wait_for(kv.at[:,0,:,0,0:2,0],f_send.at[d])
    wait_for(kv.at[:,:,:,:,:,0],c_send.at[0])
    wait_for(kv.at[:,:,:,:,:,0],c_recv.at[0])
    wait_for(qg,o_recv.at[0])

def gather(off,q,k,v,g):
    return pl.pallas_call(gather_kernel,
        out_shape=(pltpu.VMEM(KV,BF),pltpu.VMEM(QG,BF)),
        in_specs=[ANY]*5,
        out_specs=(VM,VM),
        scratch_shapes=[pltpu.VMEM((24,4,4096),BF)]*3+[pltpu.VMEM((3,8,4096),BF)]+[pltpu.VMEM((32,2,3,8,HD),BF)]*3+[
            pltpu.SMEM((HEADS,),jnp.int32),DMA((11,)),DMA((1,)),DMA((8,)),DMA((1,)),DMA((8,)),DMA((2,)),DMA((2,8)),DMA((2,)),DMA((8,)),DMA((1,)),DMA((1,)),DMA((1,)),DMA((1,))],
        name="gather",
        compiler_params=pltpu.CompilerParams(collective_id=0,has_side_effects=True,vmem_limit_bytes=40<<20))(*[afar(a) for a in (off,q,k,v,g)])

def scatter_kernel(dkv, og, o_out, dq_out, dk_out, dv_out,
                   own, far_in, near_in, last_in, og_in, fin,
                   c_send, c_recv, g_send, g_recv, far_send, far_recv, near_send, last_send, fin_recv, p_send, p_recv):
    x_lo,z,x_hi,y,c=place()
    x=x_hi*2+x_lo
    right=(x+1)%4; left=(x+3)%4; far=(x+2)%4
    mine=z*4+y
    cols=pl.ds(pl.multiple_of(mine*HD,HD),HD)
    outs=(o_out,dq_out,dk_out,dv_out)
    def at_z(i):
        return (z+order(i))%8
    greet(x,z,y,c)
    greeted()
    def back(op):
        def one(i,_):
            t=i//12; e=i%12
            blk=t*4+x+(t%2)*(3-2*x)
            tile=2*blk+(c+t)%2
            def hand(unit,count):
                piece=unit//3; k=unit%3; u=unit-tile*32
                xp=((piece//8)%2)*2+(piece//128)
                zp=(piece//16)%8; yp=(piece%8)//2; cp_=piece%2
                s=zp*4+yp
                src=og.at[t,:,pl.ds(u,count)]; dst=og_in.at[s,:,pl.ds(k,count)]
                sem=g_recv.at[zp]
                @pl.when((xp!=x)|(cp_!=c))
                def _():
                    cp=remote(src,dst,g_send.at[0],sem,device(xp,z,y,cp_))
                    if op=="start": cp.start()
                    else: cp.wait_send()
                if op=="start":
                    @pl.when((xp==x)&(cp_==c))
                    def _():
                        pltpu.make_async_copy(src,dst,sem).start()
            @pl.when(e<10)
            def _():
                hand(((tile*32+2)//3+e)*3,3)
            @pl.when(e>=10)
            def _():
                n=e-10; r=tile%3
                hand(tile*32+n+30*(1-(r+1)//2)+30*n*(r%2),1)
            return 0
        lax.fori_loop(0,36,one,0)
    for i in range(8):
        z2=at_z(i)
        remote(dkv.at[:,:,z2,:,:,1-c],own.at[:,:,z2],c_send.at[0],c_recv.at[i],device(x,z,y,1-c)).start()
    back("start")
    def to_rows(a, src, sem, s, i, j):
        dst=outs[a].at[:,:,cols]
        if isinstance(i,int) and i==0 and j==0:
            pltpu.make_async_copy(src,dst,p_recv.at[a]).start()
        else:
            remote(src,dst,sem,p_recv.at[a],device(x,s//4,s%4,c)).start()
    def sum_cores(i):
        z2=at_z(i)
        wait_for(own.at[:,:,z2],c_recv.at[i])
        for xl in range(2):
            for xh in range(2):
                own[:,xl,z2,xh]=(own[:,xl,z2,xh].astype(F32)+dkv[:,xl,z2,xh,:,c].astype(F32)).astype(BF)
        ef=own.at[:,far%2,z2,far//2]; er=own.at[:,right%2,z2,right//2]; el=own.at[:,left%2,z2,left//2]
        remote(ef.at[:,0:2],far_in.at[0,z2],far_send.at[0],far_recv.at[0,i],device(right,z,y,c)).start()
        remote(ef.at[:,2:4],far_in.at[1,z2],far_send.at[0],far_recv.at[1,i],device(left,z,y,c)).start()
        remote(er.at[:,2:4],near_in.at[0,z2],near_send.at[0],fin_recv.at[i],device(right,z,y,c)).start()
        remote(el.at[:,0:2],near_in.at[1,z2],near_send.at[0],fin_recv.at[i],device(left,z,y,c)).start()
    def rows_back(i):
        z2=at_z(i)
        wait_for(og_in.at[0:4],g_recv.at[z2])
        for j in range(4):
            s=z2*4+(y+j)%4
            to_rows(0,og_in.at[s,0],p_send.at[0],s,i,j)
            to_rows(1,og_in.at[s,1],p_send.at[0],s,i,j)
    def relay(i):
        z2=at_z(i)
        for d,peer in ((0,right),(1,left)):
            lo=2*d
            buf=far_in.at[d,z2]
            wait_for(buf,far_recv.at[d,i])
            far_in[d,z2]=(far_in[d,z2].astype(F32)+own[:,peer%2,z2,peer//2,lo:lo+2].astype(F32)).astype(BF)
            remote(buf,last_in.at[d,z2],last_send.at[0],fin_recv.at[i],device(peer,z,y,c)).start()
    def finish(i):
        z2=at_z(i)
        wait_for(own.at[:,0,z2],fin_recv.at[i])
        for d in range(2):
            lo=2*d
            fin[:,pl.ds(z2*4+lo,2)]=(own[:,x_lo,z2,x_hi,lo:lo+2].astype(F32)+last_in[d,z2].astype(F32)+near_in[1-d,z2].astype(F32)).astype(BF)
        for j in range(4):
            s=z2*4+(y+j)%4
            to_rows(2,fin.at[0,s],p_send.at[1],s,i,j)
            to_rows(3,fin.at[1,s],p_send.at[1],s,i,j)
    def loop(lo,hi,*acts):
        def body(i,_):
            for act in acts: act(i)
            return 0
        lax.fori_loop(lo,hi,body,0)
    sum_cores(0)
    rows_back(0)
    loop(1,8,sum_cores,rows_back)
    loop(0,2,relay)
    relay(2); finish(0)
    loop(3,8,relay,lambda i: finish(i-2))
    loop(6,8,finish)
    back("done")
    wait_for(own,c_send.at[0])
    for b,sem in ((far_in,far_send),(near_in,near_send),(last_in,last_send)):
        wait_for(b,sem.at[0])
    wait_for(og_in.at[0:31],p_send.at[0])
    wait_for(fin.at[:,0:31],p_send.at[1])
    for a in range(4):
        wait_for(outs[a],p_recv.at[a])

def scatter(dkv,og):
    return pl.pallas_call(scatter_kernel,
        out_shape=(pltpu.VMEM((3,8,4096),BF),)*4,
        in_specs=[VM]*2,
        out_specs=(VM,)*4,
        scratch_shapes=[pltpu.VMEM((2,2,8,2,4,3,8,HD),BF)]+[pltpu.VMEM((2,8,2,2,3,8,HD),BF)]*3+[pltpu.VMEM((32,2,3,8,HD),BF),pltpu.VMEM((2,32,3,8,HD),BF),
            DMA((1,)),DMA((8,)),DMA((1,)),DMA((8,)),DMA((1,)),DMA((2,8)),DMA((1,)),DMA((1,)),DMA((8,)),DMA((2,)),DMA((4,))],
        name="scatter",
        compiler_params=pltpu.CompilerParams(collective_id=1,has_side_effects=True,vmem_limit_bytes=40<<20))(held(dkv),held(og))

def settle_kernel(*refs):
    sem=refs[8]
    cps=[pltpu.make_async_copy(refs[i],refs[4+i],sem.at[i]) for i in range(4)]
    for cp in cps: cp.start()
    for cp in cps: cp.wait()

def settle(outs):
    return pl.pallas_call(settle_kernel,
        out_shape=(jax.ShapeDtypeStruct((3,8,4096),BF),)*4,
        in_specs=[VM]*4,out_specs=(ANY,)*4,
        scratch_shapes=[DMA((4,))],
        name="settle",
        compiler_params=pltpu.CompilerParams(vmem_limit_bytes=40<<20))(*[held(o) for o in outs])

def on_device(queries,key_states,value_states,out_grad,offsets,block_mask):
    kv,qg=gather(offsets,queries,key_states,value_states,out_grad.reshape(3,8,4096))
    dkv,og=attend(block_mask,kv,qg)
    outs=settle(scatter(dkv,og))
    return tuple(o.reshape(24,4096) for o in outs)


def solution(mesh):
    rows3=P(("ctx","head"),None,None); rows2=P(("ctx","head"),None)
    return jax.shard_map(on_device,mesh=mesh,in_specs=(rows3,rows3,rows3,rows2,P(),P()),
                         out_specs=(rows2,)*4,check_vma=False)
```

time: 108 us -> 89.3 us (0.83)
  the two profiles are of different devices: /device:TPU:1 before, /device:TPU:32 now
where the time goes in v2:
time: 89.3 us; the launch traced here: 89.1 us
  Pallas kernels  88.5 us (99%)
    pallas_call x1, Pallas kernels, scatter(): pl.pallas_call(scatter_kernel, out_shape=(pltpu.VMEM((3, 8, 4096), BF),)...  39.4 us
    pallas_call x1, Pallas kernels, gather(): pl.pallas_call(gather_kernel, out_shape=(pltpu.VMEM(KV, BF), pltpu.VMEM(Q...  34.5 us
    pallas_call x1, Pallas kernels, attend(): pl.pallas_call(attend_kernel, out_shape=(pltpu.VMEM(KV, BF), pltpu.VMEM(Q...  13.7 us

profile of v2, /device:TPU:32, one launch (start us, length us, event | category | flops | bytes accessed | tf_op | source)
XLA Modules:
  0.0 89.1 jit_solution(16848116137053093622)
XLA Ops:
  0.6 34.5 %gather.1 = (bf16[2,2,8,2,4,2,3,8,128]{8,7,6,5,4,3,2,1,0:T(8,128)(2,1)S(1)}, bf16[3,2,32,8,128]{4,3,2,1,0:T(8,128)(2,1)S(1)}) custom-call(s32[32]{0:T(128)} %off_hbm.1, bf16[24,4,4096]{2,1,0:T(4,128)(2,1)} %q.1, bf16[24,4,4096]{2,1,0:T(4,128)(2,1)} %k.1, bf16[24,4,4096]{2,1,0:T(4,128)(2,1)} %v.1, bf16[3,8,4096]{2,1,0:T(8,128)(2,1)} %bitcast.5), custom_call_target="tpu_custom_call" | custom-call | tf_op jit(solution)/shard_map/gather/pallas_call | solution.py:307
  35.1 13.7 %attend.1 = (bf16[2,2,8,2,4,2,3,8,128]{8,7,6,5,4,3,2,1,0:T(8,128)(2,1)S(1)}, bf16[3,2,32,8,128]{4,3,2,1,0:T(8,128)(2,1)S(1)}) custom-call(s32[12,12]{1,0:T(8,128)} %mask_hbm.1, bf16[2,2,8,2,4,2,3,8,128]{8,7,6,5,4,3,2,1,0:T(8,128)(2,1)S(1)} %get-tuple-element.16.kv_ref, bf16[3,2,32,8,128]{4,3,2,1,0:T(8,128)(2,1)S(1)} %get-tuple-element.17.qg_ref), custom_call_target="tpu_custom_call" | custom-call | tf_op jit(solution)/shard_map/attend/pallas_call | solution.py:127
  48.8 39.4 %scatter.1 = (bf16[3,8,4096]{2,1,0:T(8,128)(2,1)S(1)}, bf16[3,8,4096]{2,1,0:T(8,128)(2,1)S(1)}, bf16[3,8,4096]{2,1,0:T(8,128)(2,1)S(1)}, bf16[3,8,4096]{2,1,0:T(8,128)(2,1)S(1)}) custom-call(bf16[2,2,8,2,4,2,3,8,128]{8,7,6,5,4,3,2,1,0:T(8,128)(2,1)S(1)} %get-tuple-element.18.dkv, bf16[3,2,32,8,128]{4,3,2,1,0:T(8,128)(2,1)S(1)} %get-tuple-element.19.og), custom_call_target="tpu_custom_call" | custom-call | tf_op jit(solution)/shard_map/scatter/pallas_call | solution.py:427
  88.2 0.9 %settle.1 = (bf16[3,8,4096]{2,1,0:T(8,128)(2,1)}, bf16[3,8,4096]{2,1,0:T(8,128)(2,1)}, bf16[3,8,4096]{2,1,0:T(8,128)(2,1)}, bf16[3,8,4096]{2,1,0:T(8,128)(2,1)}) custom-call(bf16[3,8,4096]{2,1,0:T(8,128)(2,1)S(1)} %get-tuple-element.20.refs_0_, bf16[3,8,4096]{2,1,0:T(8,128)(2,1)S(1)} %get-tuple-element.21.refs_1_, ...), custom_call_target="tpu_custom_call" | custom-call | tf_op jit(solution)/shard_map/settle/pallas_call | solution.py:443

commit v3 on v2

--- a/solution.py
+++ b/solution.py
@@ -215,10 +215,15 @@
         for j in range(4):
             y2=(y+j)%4
             src=out.at[z2*4+y2]
-            if isinstance(i,int) and i==0 and j==0:
-                pltpu.make_async_copy(src,dst,recv).start()
+            if j:
+                remote(src,dst,send,recv,device(x,z2,y2,c)).start()
             else:
-                remote(src,dst,send,recv,device(x,z2,y2,c)).start()
+                @pl.when(z2!=z)
+                def _():
+                    remote(src,dst,send,recv,device(x,z2,y2,c)).start()
+                @pl.when(z2==z)
+                def _():
+                    pltpu.make_async_copy(src,dst,recv).start()
     def send_kv(i):
         to_plane(i,kv_out,kv.at[:,x_lo,z,x_hi,y,c],a_send.at[0],a_recv.at[i])
     def send_qg(i):
@@ -287,9 +292,9 @@
     send_kv(0)
     loop(1,8,pick_kv,send_kv)
     wait_for(q_vm,ld.at[8]); wait_for(g_vm,ld.at[9])
-    pick_qg(0); send_qg(0); ring(0)
-    loop(1,8,pick_qg,send_qg,ring)
-    loop(0,4,halves)
+    loop(0,8,pick_qg,send_qg)
+    loop(0,4,ring)
+    seq(4,8,(ring,0),(halves,-4))
     seq(4,8,(halves,0),(spread_start,-4))
     seq(0,4,(last,0),(spread_start,4))
     loop(4,8,last)
@@ -313,7 +318,7 @@
         name="gather",
         compiler_params=pltpu.CompilerParams(collective_id=0,has_side_effects=True,vmem_limit_bytes=40<<20))(*[afar(a) for a in (off,q,k,v,g)])
 
-def scatter_kernel(dkv, og, o_out, dq_out, dk_out, dv_out,
+def scatter_kernel(dkv, og, out,
                    own, far_in, near_in, last_in, og_in, fin,
                    c_send, c_recv, g_send, g_recv, far_send, far_recv, near_send, last_send, fin_recv, p_send, p_recv):
     x_lo,z,x_hi,y,c=place()
@@ -321,9 +326,8 @@
     right=(x+1)%4; left=(x+3)%4; far=(x+2)%4
     mine=z*4+y
     cols=pl.ds(pl.multiple_of(mine*HD,HD),HD)
-    outs=(o_out,dq_out,dk_out,dv_out)
     def at_z(i):
-        return (z+order(i))%8
+        return (z+order(7-i))%8
     greet(x,z,y,c)
     greeted()
     def back(op):
@@ -360,30 +364,32 @@
         z2=at_z(i)
         remote(dkv.at[:,:,z2,:,:,1-c],own.at[:,:,z2],c_send.at[0],c_recv.at[i],device(x,z,y,1-c)).start()
     back("start")
-    def to_rows(a, src, sem, s, i, j):
-        dst=outs[a].at[:,:,cols]
-        if isinstance(i,int) and i==0 and j==0:
-            pltpu.make_async_copy(src,dst,p_recv.at[a]).start()
+    def to_rows(a, src, s, j):
+        dst=out.at[2*a:2*a+2,:,:,cols]
+        def away():
+            remote(src,dst,p_send.at[a],p_recv.at[a],device(x,s//4,s%4,c)).start()
+        if j:
+            away()
         else:
-            remote(src,dst,sem,p_recv.at[a],device(x,s//4,s%4,c)).start()
+            pl.when(s!=mine)(away)
+            @pl.when(s==mine)
+            def _():
+                pltpu.make_async_copy(src,dst,p_recv.at[a]).start()
     def sum_cores(i):
         z2=at_z(i)
         wait_for(own.at[:,:,z2],c_recv.at[i])
         for xl in range(2):
             for xh in range(2):
                 own[:,xl,z2,xh]=(own[:,xl,z2,xh].astype(F32)+dkv[:,xl,z2,xh,:,c].astype(F32)).astype(BF)
-        ef=own.at[:,far%2,z2,far//2]; er=own.at[:,right%2,z2,right//2]; el=own.at[:,left%2,z2,left//2]
+        ef=own.at[:,far%2,z2,far//2]
         remote(ef.at[:,0:2],far_in.at[0,z2],far_send.at[0],far_recv.at[0,i],device(right,z,y,c)).start()
         remote(ef.at[:,2:4],far_in.at[1,z2],far_send.at[0],far_recv.at[1,i],device(left,z,y,c)).start()
-        remote(er.at[:,2:4],near_in.at[0,z2],near_send.at[0],fin_recv.at[i],device(right,z,y,c)).start()
-        remote(el.at[:,0:2],near_in.at[1,z2],near_send.at[0],fin_recv.at[i],device(left,z,y,c)).start()
     def rows_back(i):
         z2=at_z(i)
         wait_for(og_in.at[0:4],g_recv.at[z2])
         for j in range(4):
             s=z2*4+(y+j)%4
-            to_rows(0,og_in.at[s,0],p_send.at[0],s,i,j)
-            to_rows(1,og_in.at[s,1],p_send.at[0],s,i,j)
+            to_rows(0,og_in.at[s],s,j)
     def relay(i):
         z2=at_z(i)
         for d,peer in ((0,right),(1,left)):
@@ -392,6 +398,9 @@
             wait_for(buf,far_recv.at[d,i])
             far_in[d,z2]=(far_in[d,z2].astype(F32)+own[:,peer%2,z2,peer//2,lo:lo+2].astype(F32)).astype(BF)
             remote(buf,last_in.at[d,z2],last_send.at[0],fin_recv.at[i],device(peer,z,y,c)).start()
+        er=own.at[:,right%2,z2,right//2]; el=own.at[:,left%2,z2,left//2]
+        remote(er.at[:,2:4],near_in.at[0,z2],near_send.at[0],fin_recv.at[i],device(right,z,y,c)).start()
+        remote(el.at[:,0:2],near_in.at[1,z2],near_send.at[0],fin_recv.at[i],device(left,z,y,c)).start()
     def finish(i):
         z2=at_z(i)
         wait_for(own.at[:,0,z2],fin_recv.at[i])
@@ -400,52 +409,48 @@
             fin[:,pl.ds(z2*4+lo,2)]=(own[:,x_lo,z2,x_hi,lo:lo+2].astype(F32)+last_in[d,z2].astype(F32)+near_in[1-d,z2].astype(F32)).astype(BF)
         for j in range(4):
             s=z2*4+(y+j)%4
-            to_rows(2,fin.at[0,s],p_send.at[1],s,i,j)
-            to_rows(3,fin.at[1,s],p_send.at[1],s,i,j)
+            to_rows(1,fin.at[:,s],s,j)
     def loop(lo,hi,*acts):
         def body(i,_):
             for act in acts: act(i)
             return 0
         lax.fori_loop(lo,hi,body,0)
-    sum_cores(0)
-    rows_back(0)
-    loop(1,8,sum_cores,rows_back)
-    loop(0,2,relay)
-    relay(2); finish(0)
-    loop(3,8,relay,lambda i: finish(i-2))
-    loop(6,8,finish)
+    loop(0,8,sum_cores)
+    loop(0,8,rows_back)
+    loop(0,4,relay)
+    loop(4,8,relay,lambda i: finish(i-4))
+    loop(4,8,finish)
     back("done")
     wait_for(own,c_send.at[0])
     for b,sem in ((far_in,far_send),(near_in,near_send),(last_in,last_send)):
         wait_for(b,sem.at[0])
     wait_for(og_in.at[0:31],p_send.at[0])
     wait_for(fin.at[:,0:31],p_send.at[1])
-    for a in range(4):
-        wait_for(outs[a],p_recv.at[a])
+    for a in range(2):
+        wait_for(out.at[2*a:2*a+2],p_recv.at[a])
 
 def scatter(dkv,og):
     return pl.pallas_call(scatter_kernel,
-        out_shape=(pltpu.VMEM((3,8,4096),BF),)*4,
+        out_shape=pltpu.VMEM((4,3,8,4096),BF),
         in_specs=[VM]*2,
-        out_specs=(VM,)*4,
+        out_specs=VM,
         scratch_shapes=[pltpu.VMEM((2,2,8,2,4,3,8,HD),BF)]+[pltpu.VMEM((2,8,2,2,3,8,HD),BF)]*3+[pltpu.VMEM((32,2,3,8,HD),BF),pltpu.VMEM((2,32,3,8,HD),BF),
-            DMA((1,)),DMA((8,)),DMA((1,)),DMA((8,)),DMA((1,)),DMA((2,8)),DMA((1,)),DMA((1,)),DMA((8,)),DMA((2,)),DMA((4,))],
+            DMA((1,)),DMA((8,)),DMA((1,)),DMA((8,)),DMA((1,)),DMA((2,8)),DMA((1,)),DMA((1,)),DMA((8,)),DMA((2,)),DMA((2,))],
         name="scatter",
         compiler_params=pltpu.CompilerParams(collective_id=1,has_side_effects=True,vmem_limit_bytes=40<<20))(held(dkv),held(og))
 
-def settle_kernel(*refs):
-    sem=refs[8]
-    cps=[pltpu.make_async_copy(refs[i],refs[4+i],sem.at[i]) for i in range(4)]
+def settle_kernel(src,*refs):
+    cps=[pltpu.make_async_copy(src.at[i],refs[i],refs[4].at[i]) for i in range(4)]
     for cp in cps: cp.start()
     for cp in cps: cp.wait()
 
-def settle(outs):
+def settle(out):
     return pl.pallas_call(settle_kernel,
         out_shape=(jax.ShapeDtypeStruct((3,8,4096),BF),)*4,
-        in_specs=[VM]*4,out_specs=(ANY,)*4,
+        in_specs=[VM],out_specs=(ANY,)*4,
         scratch_shapes=[DMA((4,))],
         name="settle",
-        compiler_params=pltpu.CompilerParams(vmem_limit_bytes=40<<20))(*[held(o) for o in outs])
+        compiler_params=pltpu.CompilerParams(vmem_limit_bytes=40<<20))(held(out))
 
 def on_device(queries,key_states,value_states,out_grad,offsets,block_mask):
     kv,qg=gather(offsets,queries,key_states,value_states,out_grad.reshape(3,8,4096))

time: 89.3 us -> 83.6 us (0.936)
  the two profiles are of different devices: /device:TPU:32 before, /device:TPU:1 now
where the time goes in v3:
time: 83.6 us; the launch traced here: 83.5 us
  Pallas kernels  82.8 us (99%)
    pallas_call x1, Pallas kernels, gather(): pl.pallas_call(gather_kernel, out_shape=(pltpu.VMEM(KV, BF), pltpu.VMEM(Q...  35.5 us
    pallas_call x1, Pallas kernels, scatter(): pl.pallas_call(scatter_kernel, out_shape=pltpu.VMEM((4, 3, 8, 4096), BF),...  34.3 us
    pallas_call x1, Pallas kernels, attend(): pl.pallas_call(attend_kernel, out_shape=(pltpu.VMEM(KV, BF), pltpu.VMEM(Q...  12.1 us

profile of v3, /device:TPU:1, one launch (start us, length us, event | category | flops | bytes accessed | tf_op | source)
XLA Modules:
  0.0 83.5 jit_solution(7185026213229747746)
XLA Ops:
  0.6 35.5 %gather.1 = (bf16[2,2,8,2,4,2,3,8,128]{8,7,6,5,4,3,2,1,0:T(8,128)(2,1)S(1)}, bf16[3,2,32,8,128]{4,3,2,1,0:T(8,128)(2,1)S(1)}) custom-call(s32[32]{0:T(128)} %off_hbm.1, bf16[24,4,4096]{2,1,0:T(4,128)(2,1)} %q.1, bf16[24,4,4096]{2,1,0:T(4,128)(2,1)} %k.1, bf16[24,4,4096]{2,1,0:T(4,128)(2,1)} %v.1, bf16[3,8,4096]{2,1,0:T(8,128)(2,1)} %bitcast.5), custom_call_target="tpu_custom_call" | custom-call | tf_op jit(solution)/shard_map/gather/pallas_call | solution.py:312
  36.2 12.1 %attend.1 = (bf16[2,2,8,2,4,2,3,8,128]{8,7,6,5,4,3,2,1,0:T(8,128)(2,1)S(1)}, bf16[3,2,32,8,128]{4,3,2,1,0:T(8,128)(2,1)S(1)}) custom-call(s32[12,12]{1,0:T(8,128)} %mask_hbm.1, bf16[2,2,8,2,4,2,3,8,128]{8,7,6,5,4,3,2,1,0:T(8,128)(2,1)S(1)} %get-tuple-element.12.kv_ref, bf16[3,2,32,8,128]{4,3,2,1,0:T(8,128)(2,1)S(1)} %get-tuple-element.13.qg_ref), custom_call_target="tpu_custom_call" | custom-call | tf_op jit(solution)/shard_map/attend/pallas_call | solution.py:127
  48.3 34.3 %scatter.1.src = bf16[4,3,8,4096]{3,2,1,0:T(8,128)(2,1)S(1)} custom-call(bf16[2,2,8,2,4,2,3,8,128]{8,7,6,5,4,3,2,1,0:T(8,128)(2,1)S(1)} %get-tuple-element.14.dkv, bf16[3,2,32,8,128]{4,3,2,1,0:T(8,128)(2,1)S(1)} %get-tuple-element.15.og), custom_call_target="tpu_custom_call" | custom-call | tf_op jit(solution)/shard_map/scatter/pallas_call | solution.py:433
  82.6 0.9 %settle.1 = (bf16[3,8,4096]{2,1,0:T(8,128)(2,1)}, bf16[3,8,4096]{2,1,0:T(8,128)(2,1)}, bf16[3,8,4096]{2,1,0:T(8,128)(2,1)}, bf16[3,8,4096]{2,1,0:T(8,128)(2,1)}) custom-call(bf16[4,3,8,4096]{3,2,1,0:T(8,128)(2,1)S(1)} %scatter.1.src), custom_call_target="tpu_custom_call" | custom-call | tf_op jit(solution)/shard_map/settle/pallas_call | solution.py:448

commit v4 on v3

--- a/solution.py
+++ b/solution.py
@@ -7,7 +7,7 @@
 HEADS=32; NB=12; BLK=512; TQ=256; HD=128
 SCALE=HD**-0.5
 C2=SCALE*1.4426950408889634
-GF=2; GB=2
+FU=4; GB=4
 
 def dot(a,b):
     return jnp.dot(a,b,preferred_element_type=F32)
@@ -20,7 +20,7 @@
     return (hd//8)*2+ctx//8, hd%2
 
 def attend_kernel(mask_hbm, kv_ref, qg_ref, dkv_ref, og_ref,
-                  p_sc, m_sc, dk_acc, dv_acc, ot_acc, dqt_acc, live, mask_ref, ld):
+                  p_sc, m_sc, dk_acc, dv_acc, ot_acc, dqt_acc, s_sc, live, mask_ref, ld):
     grp,core=my_tiles()
     fetch=pltpu.make_async_copy(mask_hbm,mask_ref,ld.at[0])
     fetch.start()
@@ -42,43 +42,44 @@
         def count(j,n):
             live[n]=j
             return n+mask_ref[b,j]
-        n_live=lax.fori_loop(0,b,count,0)
-        def fwd(js,slots,diag,m,l):
-            ss=[]
-            for j in js:
-                s=dot(blk(0,j),qt)
-                if diag:
-                    kr=lax.broadcasted_iota(jnp.int32,(BLK,TQ),0); qc=lax.broadcasted_iota(jnp.int32,(BLK,TQ),1)+half*TQ
-                    s=jnp.where(kr<=qc,s,-1e30)
-                ss.append(s)
-            m_new=m
-            for s in ss: m_new=jnp.maximum(m_new,jnp.max(s,axis=0,keepdims=True))
-            mc=m_new*C2
-            alpha=jnp.exp2(m*C2-mc)
-            l=l*alpha
-            acc=ot_acc[...]*alpha
-            for j,slot,s in zip(js,slots,ss):
-                p=jnp.exp2(s*C2-mc)
-                pb=p.astype(BF)
-                p_sc[slot]=pb
-                m_sc[slot]=m_new
-                l=l+jnp.sum(p,axis=0,keepdims=True)
-                acc=acc+dot_t(blk(1,j),pb)
-            ot_acc[...]=acc
-            return m_new,l
-        def run(group,step,carry):
-            whole=n_live//group
-            def body(i,c):
-                idx=[i*group+e for e in range(group)]
-                return step([live[e] for e in idx],idx,c)
-            carry=lax.fori_loop(0,whole,body,carry)
-            if group>1:
-                carry=lax.fori_loop(whole*group,n_live,lambda i,c: step([live[i]],[i],c),carry)
-            return carry
+        live[0]=b
+        n_live=lax.fori_loop(0,b,count,1)
+        live[n_live]=b
+        s=dot(blk(0,b),qt)
+        kr=lax.broadcasted_iota(jnp.int32,(BLK,TQ),0); qc=lax.broadcasted_iota(jnp.int32,(BLK,TQ),1)+half*TQ
+        s=jnp.where(kr<=qc,s,-1e30)
+        s_sc[0]=s
+        def fwd(i,cur,carry):
+            m_old,l,m=carry
+            s_next=dot(blk(0,live[i+1]),qt)
+            s_sc[1-cur]=s_next
+            m_next=jnp.maximum(m,jnp.max(s_next,axis=0,keepdims=True))
+            mc=m*C2
+            alpha=jnp.exp2(m_old*C2-mc)
+            p=jnp.exp2(s_sc[cur]*C2-mc)
+            pb=p.astype(BF)
+            p_sc[i]=pb
+            m_sc[i]=m
+            l=l*alpha+jnp.sum(p,axis=0,keepdims=True)
+            ot_acc[...]=ot_acc[...]*alpha+dot_t(blk(1,live[i]),pb)
+            return m,l,m_next
         ot_acc[...]=jnp.zeros((HD,TQ),F32)
-        m=jnp.full((1,TQ),-1e30,F32); l=jnp.zeros((1,TQ),F32)
-        m,l=fwd([b],[NB-1],True,m,l)
-        m,l=run(GF,lambda js,sl,c: fwd(js,sl,False,*c),(m,l))
+        m=jnp.max(s,axis=0,keepdims=True)
+        c=(m,jnp.zeros((1,TQ),F32),m)
+        def groups(step,size,c):
+            start=0
+            while size:
+                count=(n_live-start)//size
+                def run(i,c,start=start,size=size):
+                    return step(start+i*size,size,c)
+                c=lax.fori_loop(0,count,run,c)
+                start=start+count*size
+                size//=2
+            return c
+        def fwds(i,size,c):
+            for e in range(size): c=fwd(i+e,e%2,c)
+            return c
+        m,l,_=groups(fwds,FU,c)
         inv=1.0/l
         ot=(ot_acc[...]*inv).astype(BF)
         og_ref[t,0]=ot.T.reshape(32,8,HD)
@@ -98,8 +99,10 @@
             dqt_acc[...]=acc
             return c
         dqt_acc[...]=jnp.zeros((HD,TQ),F32)
-        bwd([b],[NB-1],0)
-        run(GB,bwd,0)
+        def bwds(i,size,c):
+            idx=[i+e for e in range(size)]
+            return bwd([live[e] for e in idx],idx,c)
+        groups(bwds,GB,0)
         og_ref[t,1]=(dqt_acc[...]*SCALE).astype(BF).T.reshape(32,8,HD)
     def settle_blocks(lo,hi):
         @pl.loop(lo,hi)
@@ -130,7 +133,7 @@
         out_specs=(VM,VM),
         scratch_shapes=[
             pltpu.VMEM((NB,BLK,TQ),BF),pltpu.VMEM((NB,1,TQ),F32),pltpu.VMEM((NB*BLK,HD),F32),pltpu.VMEM((NB*BLK,HD),F32),
-            pltpu.VMEM((HD,TQ),F32),pltpu.VMEM((HD,TQ),F32),pltpu.SMEM((16,),jnp.int32),pltpu.SMEM((NB,NB),jnp.int32),DMA((1,))],
+            pltpu.VMEM((HD,TQ),F32),pltpu.VMEM((HD,TQ),F32),pltpu.VMEM((2,BLK,TQ),F32),pltpu.SMEM((16,),jnp.int32),pltpu.SMEM((NB,NB),jnp.int32),DMA((1,))],
         name="attend",
         compiler_params=pltpu.CompilerParams(vmem_limit_bytes=40<<20))(afar(mask),held(kv),held(qg))
 

time: 83.6 us -> 79 us (0.945)
  Pallas kernels: 82.8 us -> 78.2 us
    pallas_call x1, Pallas kernels: 34.3 us -> 31.2 us  [scatter(): pl.pallas_call(scatter_kernel, out_shape=pltpu.VMEM((4, 3, 8, 4096), BF),...]
    pallas_call x1, Pallas kernels: 12.1 us -> 10.5 us  [attend(): pl.pallas_call(attend_kernel, out_shape=(pltpu.VMEM(KV, BF), pltpu.VMEM(Q...]
where the time goes in v4:
time: 79 us; the launch traced here: 78.8 us
  Pallas kernels  78.2 us (99%)
    pallas_call x1, Pallas kernels, gather(): pl.pallas_call(gather_kernel, out_shape=(pltpu.VMEM(KV, BF), pltpu.VMEM(Q...  35.5 us
    pallas_call x1, Pallas kernels, scatter(): pl.pallas_call(scatter_kernel, out_shape=pltpu.VMEM((4, 3, 8, 4096), BF),...  31.2 us
    pallas_call x1, Pallas kernels, attend(): pl.pallas_call(attend_kernel, out_shape=(pltpu.VMEM(KV, BF), pltpu.VMEM(Q...  10.5 us

profile of v4, /device:TPU:1, one launch (start us, length us, event | category | flops | bytes accessed | tf_op | source)
XLA Modules:
  0.0 78.8 jit_solution(10569234630062630106)
XLA Ops:
  0.6 35.5 %gather.1 = (bf16[2,2,8,2,4,2,3,8,128]{8,7,6,5,4,3,2,1,0:T(8,128)(2,1)S(1)}, bf16[3,2,32,8,128]{4,3,2,1,0:T(8,128)(2,1)S(1)}) custom-call(s32[32]{0:T(128)} %off_hbm.1, bf16[24,4,4096]{2,1,0:T(4,128)(2,1)} %q.1, bf16[24,4,4096]{2,1,0:T(4,128)(2,1)} %k.1, bf16[24,4,4096]{2,1,0:T(4,128)(2,1)} %v.1, bf16[3,8,4096]{2,1,0:T(8,128)(2,1)} %bitcast.5), custom_call_target="tpu_custom_call" | custom-call | tf_op jit(solution)/shard_map/gather/pallas_call | solution.py:315
  36.2 10.5 %attend.1 = (bf16[2,2,8,2,4,2,3,8,128]{8,7,6,5,4,3,2,1,0:T(8,128)(2,1)S(1)}, bf16[3,2,32,8,128]{4,3,2,1,0:T(8,128)(2,1)S(1)}) custom-call(s32[12,12]{1,0:T(8,128)} %mask_hbm.1, bf16[2,2,8,2,4,2,3,8,128]{8,7,6,5,4,3,2,1,0:T(8,128)(2,1)S(1)} %get-tuple-element.12.kv_ref, bf16[3,2,32,8,128]{4,3,2,1,0:T(8,128)(2,1)S(1)} %get-tuple-element.13.qg_ref), custom_call_target="tpu_custom_call" | custom-call | tf_op jit(solution)/shard_map/attend/pallas_call | solution.py:130
  46.7 31.2 %scatter.1.src = bf16[4,3,8,4096]{3,2,1,0:T(8,128)(2,1)S(1)} custom-call(bf16[2,2,8,2,4,2,3,8,128]{8,7,6,5,4,3,2,1,0:T(8,128)(2,1)S(1)} %get-tuple-element.14.dkv, bf16[3,2,32,8,128]{4,3,2,1,0:T(8,128)(2,1)S(1)} %get-tuple-element.15.og), custom_call_target="tpu_custom_call" | custom-call | tf_op jit(solution)/shard_map/scatter/pallas_call | solution.py:436
  77.9 0.9 %settle.1 = (bf16[3,8,4096]{2,1,0:T(8,128)(2,1)}, bf16[3,8,4096]{2,1,0:T(8,128)(2,1)}, bf16[3,8,4096]{2,1,0:T(8,128)(2,1)}, bf16[3,8,4096]{2,1,0:T(8,128)(2,1)}) custom-call(bf16[4,3,8,4096]{3,2,1,0:T(8,128)(2,1)S(1)} %scatter.1.src), custom_call_target="tpu_custom_call" | custom-call | tf_op jit(solution)/shard_map/settle/pallas_call | solution.py:451

commit v5 on v3

--- a/solution.py
+++ b/solution.py
@@ -7,7 +7,7 @@
 HEADS=32; NB=12; BLK=512; TQ=256; HD=128
 SCALE=HD**-0.5
 C2=SCALE*1.4426950408889634
-GF=2; GB=2
+FU=4; GB=4
 
 def dot(a,b):
     return jnp.dot(a,b,preferred_element_type=F32)
@@ -20,7 +20,7 @@
     return (hd//8)*2+ctx//8, hd%2
 
 def attend_kernel(mask_hbm, kv_ref, qg_ref, dkv_ref, og_ref,
-                  p_sc, m_sc, dk_acc, dv_acc, ot_acc, dqt_acc, live, mask_ref, ld):
+                  p_sc, m_sc, dk_acc, dv_acc, ot_acc, dqt_acc, s_sc, qt_sc, gt_sc, st_sc, live, pair_tile, mask_ref, ld):
     grp,core=my_tiles()
     fetch=pltpu.make_async_copy(mask_hbm,mask_ref,ld.at[0])
     fetch.start()
@@ -33,74 +33,87 @@
         z=jnp.zeros((BLK,HD),F32)
         rows=pl.ds(pl.multiple_of(j*BLK,BLK),BLK)
         dk_acc[rows]=z; dv_acc[rows]=z
-    def tile(t):
-        bm=grp
-        b=t*4+bm+(t%2)*(3-2*bm)
-        half=(core+t)%2
-        q=qg_ref[t,0].reshape(TQ,HD); g=qg_ref[t,1].reshape(TQ,HD)
-        qt=q.T; gt=g.T
-        def count(j,n):
-            live[n]=j
-            return n+mask_ref[b,j]
-        n_live=lax.fori_loop(0,b,count,0)
-        def fwd(js,slots,diag,m,l):
-            ss=[]
-            for j in js:
-                s=dot(blk(0,j),qt)
-                if diag:
-                    kr=lax.broadcasted_iota(jnp.int32,(BLK,TQ),0); qc=lax.broadcasted_iota(jnp.int32,(BLK,TQ),1)+half*TQ
-                    s=jnp.where(kr<=qc,s,-1e30)
-                ss.append(s)
-            m_new=m
-            for s in ss: m_new=jnp.maximum(m_new,jnp.max(s,axis=0,keepdims=True))
-            mc=m_new*C2
-            alpha=jnp.exp2(m*C2-mc)
-            l=l*alpha
-            acc=ot_acc[...]*alpha
-            for j,slot,s in zip(js,slots,ss):
-                p=jnp.exp2(s*C2-mc)
-                pb=p.astype(BF)
-                p_sc[slot]=pb
-                m_sc[slot]=m_new
-                l=l+jnp.sum(p,axis=0,keepdims=True)
-                acc=acc+dot_t(blk(1,j),pb)
-            ot_acc[...]=acc
-            return m_new,l
-        def run(group,step,carry):
-            whole=n_live//group
-            def body(i,c):
-                idx=[i*group+e for e in range(group)]
-                return step([live[e] for e in idx],idx,c)
-            carry=lax.fori_loop(0,whole,body,carry)
-            if group>1:
-                carry=lax.fori_loop(whole*group,n_live,lambda i,c: step([live[i]],[i],c),carry)
-            return carry
-        ot_acc[...]=jnp.zeros((HD,TQ),F32)
-        m=jnp.full((1,TQ),-1e30,F32); l=jnp.zeros((1,TQ),F32)
-        m,l=fwd([b],[NB-1],True,m,l)
-        m,l=run(GF,lambda js,sl,c: fwd(js,sl,False,*c),(m,l))
-        inv=1.0/l
-        ot=(ot_acc[...]*inv).astype(BF)
-        og_ref[t,0]=ot.T.reshape(32,8,HD)
-        r=jnp.sum(gt.astype(F32)*ot.astype(F32),axis=0,keepdims=True)
+    def groups(first,n_live,step,size,c):
+        start=first
+        while size:
+            count=(n_live-start)//size
+            def run(i,c,start=start,size=size):
+                return step(start+i*size,size,c)
+            c=lax.fori_loop(0,count,run,c)
+            start=start+count*size
+            size//=2
+        return c
+    def tile_of(t):
+        return t*4+grp+(t%2)*(3-2*grp), (core+t)%2
+    def note(n,t,j):
+        live[n]=j
+        pair_tile[n]=t
+    def list_blocks(t,n):
+        def one(j,n):
+            note(n,t,j)
+            return n+mask_ref[tile_of(t)[0],j]
+        return lax.fori_loop(0,tile_of(t)[0],one,n)
+    def exps(t,slot,s,m_old,m):
         mc=m*C2
-        def bwd(js,slots,c):
-            acc=dqt_acc[...]
-            for j,slot in zip(js,slots):
-                f=jnp.exp2(m_sc[slot]*C2-mc)*inv
-                p=p_sc[slot].astype(F32)*f
-                dp=dot(blk(1,j),gt)
-                ds=(p*(dp-r)).astype(BF)
-                rows=pl.ds(pl.multiple_of(j*BLK,BLK),BLK)
-                dv_acc[rows]+=dot(p.astype(BF),g)
-                dk_acc[rows]+=dot(ds,q)
-                acc=acc+dot_t(blk(0,j),ds)
-            dqt_acc[...]=acc
-            return c
-        dqt_acc[...]=jnp.zeros((HD,TQ),F32)
-        bwd([b],[NB-1],0)
-        run(GB,bwd,0)
-        og_ref[t,1]=(dqt_acc[...]*SCALE).astype(BF).T.reshape(32,8,HD)
+        alpha=jnp.exp2(m_old*C2-mc)
+        p=jnp.exp2(s*C2-mc)
+        pb=p.astype(BF)
+        p_sc[slot]=pb
+        m_sc[slot]=m
+        return alpha,jnp.sum(p,axis=0,keepdims=True),pb
+    def diagonals():
+        for t in range(3):
+            qt_sc[t]=qg_ref[t,0].reshape(TQ,HD).T
+            gt_sc[t]=qg_ref[t,1].reshape(TQ,HD).T
+        for t in range(3):
+            b,half=tile_of(t)
+            s=dot(blk(0,b),qt_sc[t])
+            kr=lax.broadcasted_iota(jnp.int32,(BLK,TQ),0); qc=lax.broadcasted_iota(jnp.int32,(BLK,TQ),1)+half*TQ
+            s=jnp.where(kr<=qc,s,-1e30)
+            m=jnp.max(s,axis=0,keepdims=True)
+            _,l,pb=exps(t,t,s,m,m)
+            st_sc[t,0]=m; st_sc[t,1]=l; st_sc[t,2]=m
+            ot_acc[t]=dot_t(blk(1,b),pb)
+    def ahead(i,slot):
+        t=pair_tile[i]
+        s=dot(blk(0,live[i]),qt_sc[t])
+        s_sc[slot]=s
+        m=jnp.maximum(st_sc[t,2],jnp.max(s,axis=0,keepdims=True))
+        st_sc[t,2]=m
+        return m
+    def fwd(i,cur,m):
+        m_next=ahead(i+1,1-cur)
+        t=pair_tile[i]
+        alpha,total,pb=exps(t,i,s_sc[cur],st_sc[t,0],m)
+        st_sc[t,0]=m
+        st_sc[t,1]=st_sc[t,1]*alpha+total
+        ot_acc[t]=ot_acc[t]*alpha+dot_t(blk(1,live[i]),pb)
+        return m_next
+    def fwds(i,size,m):
+        for e in range(size): m=fwd(i+e,(e+1)%2,m)
+        return m
+    def finish():
+        for t in range(3):
+            inv=1.0/st_sc[t,1]
+            ot=(ot_acc[t]*inv).astype(BF)
+            og_ref[t,0]=ot.T.reshape(32,8,HD)
+            st_sc[t,0]=st_sc[t,0]*C2
+            st_sc[t,1]=inv
+            st_sc[t,2]=jnp.sum(gt_sc[t].astype(F32)*ot.astype(F32),axis=0,keepdims=True)
+            dqt_acc[t]=jnp.zeros((HD,TQ),F32)
+    def bwd(i,size,c):
+        for e in range(size):
+            slot=i+e; j=live[slot]; t=pair_tile[slot]
+            gt=gt_sc[t]; q=qg_ref[t,0].reshape(TQ,HD); g=qg_ref[t,1].reshape(TQ,HD)
+            f=jnp.exp2(m_sc[slot]*C2-st_sc[t,0])*st_sc[t,1]
+            p=p_sc[slot].astype(F32)*f
+            dp=dot(blk(1,j),gt)
+            ds=(p*(dp-st_sc[t,2])).astype(BF)
+            rows=pl.ds(pl.multiple_of(j*BLK,BLK),BLK)
+            dv_acc[rows]+=dot(p.astype(BF),g)
+            dk_acc[rows]+=dot(ds,q)
+            dqt_acc[t]+=dot_t(blk(0,j),ds)
+        return c
     def settle_blocks(lo,hi):
         @pl.loop(lo,hi)
         def _(j):
@@ -108,10 +121,17 @@
             un=pl.ds(pl.multiple_of(j*64,64),64)
             dkv_rows[0,un]=(dk_acc[rows]*SCALE).astype(BF).reshape(64,8,HD)
             dkv_rows[1,un]=dv_acc[rows].astype(BF).reshape(64,8,HD)
+    diagonals()
     fetch.wait()
-    @pl.loop(0,3)
-    def _(t):
-        tile(t)
+    for t in range(3): note(t,t,tile_of(t)[0])
+    pairs=3
+    for t in range(3): pairs=list_blocks(t,pairs)
+    note(pairs,0,0)
+    groups(3,pairs,fwds,FU,ahead(3,1))
+    finish()
+    groups(0,pairs,bwd,GB,0)
+    for t in range(3):
+        og_ref[t,1]=(dqt_acc[t]*SCALE).astype(BF).T.reshape(32,8,HD)
     settle_blocks(0,NB)
 
 KV=(2,2,8,2,4,2,3,8,HD)
@@ -129,8 +149,8 @@
         in_specs=[ANY,VM,VM],
         out_specs=(VM,VM),
         scratch_shapes=[
-            pltpu.VMEM((NB,BLK,TQ),BF),pltpu.VMEM((NB,1,TQ),F32),pltpu.VMEM((NB*BLK,HD),F32),pltpu.VMEM((NB*BLK,HD),F32),
-            pltpu.VMEM((HD,TQ),F32),pltpu.VMEM((HD,TQ),F32),pltpu.SMEM((16,),jnp.int32),pltpu.SMEM((NB,NB),jnp.int32),DMA((1,))],
+            pltpu.VMEM((3*NB,BLK,TQ),BF),pltpu.VMEM((3*NB,1,TQ),F32),pltpu.VMEM((NB*BLK,HD),F32),pltpu.VMEM((NB*BLK,HD),F32),
+            pltpu.VMEM((3,HD,TQ),F32),pltpu.VMEM((3,HD,TQ),F32),pltpu.VMEM((2,BLK,TQ),F32),pltpu.VMEM((3,HD,TQ),BF),pltpu.VMEM((3,HD,TQ),BF),pltpu.VMEM((3,3,1,TQ),F32),pltpu.SMEM((3*NB+1,),jnp.int32),pltpu.SMEM((3*NB+1,),jnp.int32),pltpu.SMEM((NB,NB),jnp.int32),DMA((1,))],
         name="attend",
         compiler_params=pltpu.CompilerParams(vmem_limit_bytes=40<<20))(afar(mask),held(kv),held(qg))
 
@@ -177,6 +197,7 @@
     x=x_hi*2+x_lo
     right=(x+1)%4; left=(x+3)%4; far=(x+2)%4
     mine=z*4+y
+    greet(x,z,y,c)
     for i in range(8):
         cols=pl.ds(pl.multiple_of(((z+order(i))%8)*512,512),512)
         pltpu.make_async_copy(k.at[:,:,cols],k_vm.at[:,:,cols],ld.at[i]).start()
@@ -185,7 +206,6 @@
     pltpu.make_async_copy(g,g_vm,ld.at[9]).start()
     fetch=pltpu.make_async_copy(off_hbm,off,ld.at[10])
     fetch.start()
-    greet(x,z,y,c)
     row=lax.broadcasted_iota(jnp.int32,(24,96),0); col=lax.broadcasted_iota(jnp.int32,(24,96),1)
     lead=col-row*4
     def columns(h):

time: 83.6 us -> 78.1 us (0.934)
  Pallas kernels: 82.8 us -> 77.6 us
    pallas_call x1, Pallas kernels: 34.3 us -> 31.2 us  [scatter(): pl.pallas_call(scatter_kernel, out_shape=pltpu.VMEM((4, 3, 8, 4096), BF),...]
    pallas_call x1, Pallas kernels: 12.1 us -> 10.1 us  [attend(): pl.pallas_call(attend_kernel, out_shape=(pltpu.VMEM(KV, BF), pltpu.VMEM(Q...]
where the time goes in v5:
time: 78.1 us; the launch traced here: 78.3 us
  Pallas kernels  77.6 us (99%)
    pallas_call x1, Pallas kernels, gather(): pl.pallas_call(gather_kernel, out_shape=(pltpu.VMEM(KV, BF), pltpu.VMEM(Q...  35.5 us
    pallas_call x1, Pallas kernels, scatter(): pl.pallas_call(scatter_kernel, out_shape=pltpu.VMEM((4, 3, 8, 4096), BF),...  31.2 us
    pallas_call x1, Pallas kernels, attend(): pl.pallas_call(attend_kernel, out_shape=(pltpu.VMEM(KV, BF), pltpu.VMEM(Q...  10.1 us

profile of v5, /device:TPU:1, one launch (start us, length us, event | category | flops | bytes accessed | tf_op | source)
XLA Modules:
  0.0 78.3 jit_solution(8968797257161620600)
XLA Ops:
  0.6 35.5 %gather.1 = (bf16[2,2,8,2,4,2,3,8,128]{8,7,6,5,4,3,2,1,0:T(8,128)(2,1)S(1)}, bf16[3,2,32,8,128]{4,3,2,1,0:T(8,128)(2,1)S(1)}) custom-call(s32[32]{0:T(128)} %off_hbm.1, bf16[24,4,4096]{2,1,0:T(4,128)(2,1)} %q.1, bf16[24,4,4096]{2,1,0:T(4,128)(2,1)} %k.1, bf16[24,4,4096]{2,1,0:T(4,128)(2,1)} %v.1, bf16[3,8,4096]{2,1,0:T(8,128)(2,1)} %bitcast.5), custom_call_target="tpu_custom_call" | custom-call | tf_op jit(solution)/shard_map/gather/pallas_call | solution.py:332
  36.1 10.1 %attend.1 = (bf16[2,2,8,2,4,2,3,8,128]{8,7,6,5,4,3,2,1,0:T(8,128)(2,1)S(1)}, bf16[3,2,32,8,128]{4,3,2,1,0:T(8,128)(2,1)S(1)}) custom-call(s32[12,12]{1,0:T(8,128)} %mask_hbm.1, bf16[2,2,8,2,4,2,3,8,128]{8,7,6,5,4,3,2,1,0:T(8,128)(2,1)S(1)} %get-tuple-element.12.kv_ref, bf16[3,2,32,8,128]{4,3,2,1,0:T(8,128)(2,1)S(1)} %get-tuple-element.13.qg_ref), custom_call_target="tpu_custom_call" | custom-call | tf_op jit(solution)/shard_map/attend/pallas_call | solution.py:147
  46.2 31.2 %scatter.1.src = bf16[4,3,8,4096]{3,2,1,0:T(8,128)(2,1)S(1)} custom-call(bf16[2,2,8,2,4,2,3,8,128]{8,7,6,5,4,3,2,1,0:T(8,128)(2,1)S(1)} %get-tuple-element.14.dkv, bf16[3,2,32,8,128]{4,3,2,1,0:T(8,128)(2,1)S(1)} %get-tuple-element.15.og), custom_call_target="tpu_custom_call" | custom-call | tf_op jit(solution)/shard_map/scatter/pallas_call | solution.py:453
  77.4 0.9 %settle.1 = (bf16[3,8,4096]{2,1,0:T(8,128)(2,1)}, bf16[3,8,4096]{2,1,0:T(8,128)(2,1)}, bf16[3,8,4096]{2,1,0:T(8,128)(2,1)}, bf16[3,8,4096]{2,1,0:T(8,128)(2,1)}) custom-call(bf16[4,3,8,4096]{3,2,1,0:T(8,128)(2,1)S(1)} %scatter.1.src), custom_call_target="tpu_custom_call" | custom-call | tf_op jit(solution)/shard_map/settle/pallas_call | solution.py:468

commit v6 on v5

--- a/solution.py
+++ b/solution.py
@@ -14,6 +14,16 @@
 
 def dot_t(a,b):
     return lax.dot_general(a,b,(((0,),(0,)),((),())),preferred_element_type=F32)
+
+def entry(table,k):
+    return table//((1+3*(k%2))*(1+15*(k//2)))%4
+
+def block_of(x,t):
+    return t*4+entry(228+(75-228)*(t%2)+(54-228)*(t//2),x)
+
+def chip_of(blk):
+    t=blk//4
+    return entry(228+(30-228)*(t%2)+(135-228)*(t//2),blk%4)
 
 def my_tiles():
     ctx=lax.axis_index("ctx"); hd=lax.axis_index("head")
@@ -44,7 +54,7 @@
             size//=2
         return c
     def tile_of(t):
-        return t*4+grp+(t%2)*(3-2*grp), (core+t)%2
+        return block_of(grp,t), (core+t)%2
     def note(n,t,j):
         live[n]=j
         pair_tile[n]=t
@@ -164,8 +174,8 @@
     return ((x%2)*8+z, (x//2)*8+y*2+c)
 
 def owner(tile):
-    blk=tile//2; t=blk//4; bm=blk%4
-    return bm+(t%2)*(3-2*bm), (tile%2+t)%2, t
+    blk=tile//2; t=blk//4
+    return chip_of(blk), (tile%2+t)%2, t
 
 def order(i):
     return (i%2)*((i+1)//2)+(1-i%2)*((8-i//2)%8)
@@ -353,7 +363,7 @@
     def back(op):
         def one(i,_):
             t=i//12; e=i%12
-            blk=t*4+x+(t%2)*(3-2*x)
+            blk=block_of(x,t)
             tile=2*blk+(c+t)%2
             def hand(unit,count):
                 piece=unit//3; k=unit%3; u=unit-tile*32

time: 78.1 us -> 78.6 us (level); the launches traced: 78.3 us -> 77.6 us
    pallas_call x1, Pallas kernels: 10.1 us -> 8.34 us  [attend(): pl.pallas_call(attend_kernel, out_shape=(pltpu.VMEM(KV, BF), pltpu.VMEM(Q...]
    pallas_call x1, Pallas kernels: 31.2 us -> 32.3 us  [scatter(): pl.pallas_call(scatter_kernel, out_shape=pltpu.VMEM((4, 3, 8, 4096), BF),...]
where the time goes in v6:
time: 78.6 us; the launch traced here: 77.6 us
  Pallas kernels  77 us (98%)
    pallas_call x1, Pallas kernels, gather(): pl.pallas_call(gather_kernel, out_shape=(pltpu.VMEM(KV, BF), pltpu.VMEM(Q...  35.4 us
    pallas_call x1, Pallas kernels, scatter(): pl.pallas_call(scatter_kernel, out_shape=pltpu.VMEM((4, 3, 8, 4096), BF),...  32.3 us
    pallas_call x1, Pallas kernels, attend(): pl.pallas_call(attend_kernel, out_shape=(pltpu.VMEM(KV, BF), pltpu.VMEM(Q...  8.34 us

profile of v6, /device:TPU:1, one launch (start us, length us, event | category | flops | bytes accessed | tf_op | source)
XLA Modules:
  0.0 77.6 jit_solution(17843049278846878128)
XLA Ops:
  0.6 35.4 %gather.1 = (bf16[2,2,8,2,4,2,3,8,128]{8,7,6,5,4,3,2,1,0:T(8,128)(2,1)S(1)}, bf16[3,2,32,8,128]{4,3,2,1,0:T(8,128)(2,1)S(1)}) custom-call(s32[32]{0:T(128)} %off_hbm.1, bf16[24,4,4096]{2,1,0:T(4,128)(2,1)} %q.1, bf16[24,4,4096]{2,1,0:T(4,128)(2,1)} %k.1, bf16[24,4,4096]{2,1,0:T(4,128)(2,1)} %v.1, bf16[3,8,4096]{2,1,0:T(8,128)(2,1)} %bitcast.5), custom_call_target="tpu_custom_call" | custom-call | tf_op jit(solution)/shard_map/gather/pallas_call | solution.py:342
  36.0 8.3 %attend.1 = (bf16[2,2,8,2,4,2,3,8,128]{8,7,6,5,4,3,2,1,0:T(8,128)(2,1)S(1)}, bf16[3,2,32,8,128]{4,3,2,1,0:T(8,128)(2,1)S(1)}) custom-call(s32[12,12]{1,0:T(8,128)} %mask_hbm.1, bf16[2,2,8,2,4,2,3,8,128]{8,7,6,5,4,3,2,1,0:T(8,128)(2,1)S(1)} %get-tuple-element.12.kv_ref, bf16[3,2,32,8,128]{4,3,2,1,0:T(8,128)(2,1)S(1)} %get-tuple-element.13.qg_ref), custom_call_target="tpu_custom_call" | custom-call | tf_op jit(solution)/shard_map/attend/pallas_call | solution.py:157
  44.4 32.3 %scatter.1.src = bf16[4,3,8,4096]{3,2,1,0:T(8,128)(2,1)S(1)} custom-call(bf16[2,2,8,2,4,2,3,8,128]{8,7,6,5,4,3,2,1,0:T(8,128)(2,1)S(1)} %get-tuple-element.14.dkv, bf16[3,2,32,8,128]{4,3,2,1,0:T(8,128)(2,1)S(1)} %get-tuple-element.15.og), custom_call_target="tpu_custom_call" | custom-call | tf_op jit(solution)/shard_map/scatter/pallas_call | solution.py:463
  76.7 0.9 %settle.1 = (bf16[3,8,4096]{2,1,0:T(8,128)(2,1)}, bf16[3,8,4096]{2,1,0:T(8,128)(2,1)}, bf16[3,8,4096]{2,1,0:T(8,128)(2,1)}, bf16[3,8,4096]{2,1,0:T(8,128)(2,1)}) custom-call(bf16[4,3,8,4096]{3,2,1,0:T(8,128)(2,1)S(1)} %scatter.1.src), custom_call_target="tpu_custom_call" | custom-call | tf_op jit(solution)/shard_map/settle/pallas_call | solution.py:478

commit v7 on v6

--- a/solution.py
+++ b/solution.py
@@ -7,7 +7,7 @@
 HEADS=32; NB=12; BLK=512; TQ=256; HD=128
 SCALE=HD**-0.5
 C2=SCALE*1.4426950408889634
-FU=4; GB=4
+FU=4; GB=8
 
 def dot(a,b):
     return jnp.dot(a,b,preferred_element_type=F32)
@@ -446,10 +446,10 @@
             return 0
         lax.fori_loop(lo,hi,body,0)
     loop(0,8,sum_cores)
-    loop(0,8,rows_back)
-    loop(0,4,relay)
-    loop(4,8,relay,lambda i: finish(i-4))
-    loop(4,8,finish)
+    loop(0,2,rows_back)
+    loop(0,6,relay,lambda i: rows_back(i+2))
+    loop(6,8,relay)
+    loop(0,8,finish)
     back("done")
     wait_for(own,c_send.at[0])
     for b,sem in ((far_in,far_send),(near_in,near_send),(last_in,last_send)):

time: 78.6 us -> 78.9 us (level)
  no operation moved by 1% of the time
where the time goes in v7:
time: 78.9 us; the launch traced here: 77.9 us
  Pallas kernels  77.3 us (98%)
    pallas_call x1, Pallas kernels, gather(): pl.pallas_call(gather_kernel, out_shape=(pltpu.VMEM(KV, BF), pltpu.VMEM(Q...  35.4 us
    pallas_call x1, Pallas kernels, scatter(): pl.pallas_call(scatter_kernel, out_shape=pltpu.VMEM((4, 3, 8, 4096), BF),...  32.2 us
    pallas_call x1, Pallas kernels, attend(): pl.pallas_call(attend_kernel, out_shape=(pltpu.VMEM(KV, BF), pltpu.VMEM(Q...  8.79 us

profile of v7, /device:TPU:1, one launch (start us, length us, event | category | flops | bytes accessed | tf_op | source)
XLA Modules:
  0.0 77.9 jit_solution(4777765558521422234)
XLA Ops:
  0.6 35.4 %gather.1 = (bf16[2,2,8,2,4,2,3,8,128]{8,7,6,5,4,3,2,1,0:T(8,128)(2,1)S(1)}, bf16[3,2,32,8,128]{4,3,2,1,0:T(8,128)(2,1)S(1)}) custom-call(s32[32]{0:T(128)} %off_hbm.1, bf16[24,4,4096]{2,1,0:T(4,128)(2,1)} %q.1, bf16[24,4,4096]{2,1,0:T(4,128)(2,1)} %k.1, bf16[24,4,4096]{2,1,0:T(4,128)(2,1)} %v.1, bf16[3,8,4096]{2,1,0:T(8,128)(2,1)} %bitcast.5), custom_call_target="tpu_custom_call" | custom-call | tf_op jit(solution)/shard_map/gather/pallas_call | solution.py:342
  36.0 8.8 %attend.1 = (bf16[2,2,8,2,4,2,3,8,128]{8,7,6,5,4,3,2,1,0:T(8,128)(2,1)S(1)}, bf16[3,2,32,8,128]{4,3,2,1,0:T(8,128)(2,1)S(1)}) custom-call(s32[12,12]{1,0:T(8,128)} %mask_hbm.1, bf16[2,2,8,2,4,2,3,8,128]{8,7,6,5,4,3,2,1,0:T(8,128)(2,1)S(1)} %get-tuple-element.12.kv_ref, bf16[3,2,32,8,128]{4,3,2,1,0:T(8,128)(2,1)S(1)} %get-tuple-element.13.qg_ref), custom_call_target="tpu_custom_call" | custom-call | tf_op jit(solution)/shard_map/attend/pallas_call | solution.py:157
  44.8 32.2 %scatter.1.src = bf16[4,3,8,4096]{3,2,1,0:T(8,128)(2,1)S(1)} custom-call(bf16[2,2,8,2,4,2,3,8,128]{8,7,6,5,4,3,2,1,0:T(8,128)(2,1)S(1)} %get-tuple-element.14.dkv, bf16[3,2,32,8,128]{4,3,2,1,0:T(8,128)(2,1)S(1)} %get-tuple-element.15.og), custom_call_target="tpu_custom_call" | custom-call | tf_op jit(solution)/shard_map/scatter/pallas_call | solution.py:463
  77.0 0.9 %settle.1 = (bf16[3,8,4096]{2,1,0:T(8,128)(2,1)}, bf16[3,8,4096]{2,1,0:T(8,128)(2,1)}, bf16[3,8,4096]{2,1,0:T(8,128)(2,1)}, bf16[3,8,4096]{2,1,0:T(8,128)(2,1)}) custom-call(bf16[4,3,8,4096]{3,2,1,0:T(8,128)(2,1)S(1)} %scatter.1.src), custom_call_target="tpu_custom_call" | custom-call | tf_op jit(solution)/shard_map/settle/pallas_call | solution.py:478
